TPU v7x, 128 devices: a whole 4x4x4 slice. The times are simulated.
128 devices in a mesh: lat: 4 (over z_lo, core), lon: 32 (over x, y, z_hi).
Axes of the slice: x: 4, y: 4, z: 4 (z_hi: 2, z_lo: 2; z = z_hi * 2 + z_lo), core: 2. Of those that a mesh axis runs over, the one named last changes fastest.
Arguments:
- field: bfloat16 [512, 1024, 256], P('lat', 'lon'), may hold values from -6 to 6
- norm_gain: float32 [256], replicated, may hold values from 0.1 to 1.9
- expand_weight: bfloat16 [256, 1024], replicated, may hold values from -0.375 to 0.375
- expand_bias: float32 [1024], replicated, may hold values from -3 to 3
- depth_kernel: float32 [3, 3, 1024], replicated, may hold values from -2 to 2
- depth_bias: float32 [1024], replicated, may hold values from -3 to 3
- project_weight: bfloat16 [1024, 256], replicated, may hold values from -0.1875 to 0.1875
- block_gain: float32 [256], replicated, may hold values from 0.1 to 1.9
- block_qkv: bfloat16 [256, 768], replicated, may hold values from -0.375 to 0.375
- block_out: bfloat16 [256, 256], replicated, may hold values from -0.375 to 0.375
- grid_gain: float32 [256], replicated, may hold values from 0.1 to 1.9
- grid_qkv: bfloat16 [256, 768], replicated, may hold values from -0.375 to 0.375
- grid_out: bfloat16 [256, 256], replicated, may hold values from -0.375 to 0.375
Outputs:
- result: bfloat16 [512, 1024, 256], P('lat', 'lon')
All inputs are finite; a program needn't handle non-finite values.
Results may differ from a plain program's by a relative error of at most 0.012.
Values may be sent and summed in bfloat16 or wider, within the bound.
No kernel may reach another device: no remote copies, remote signals or barrier semaphores. Data moves between devices by JAX's collectives and lax.ppermute only.
A program may use at most 128 MiB of HBM per device.

v0:
```python
import functools
import math

import jax
import jax.numpy as jnp
from jax import lax
from jax.experimental import pallas as pl
from jax.experimental.pallas import tpu as pltpu
from jax.sharding import Mesh
from jax.sharding import PartitionSpec as P

HEADS = 8
WIDTH = 256
HEAD = WIDTH // HEADS
WIDE = 1024
COLS = 32
SLICE = 256
PARTS = 2
F32 = jnp.float32
BF16 = jnp.bfloat16
VMEM_LIMIT = 56 * 1024 * 1024


def norm_rows(values, gain):
    mean = jnp.mean(values, axis=-1, keepdims=True)
    centred = values - mean
    var = jnp.mean(centred * centred, axis=-1, keepdims=True)
    return centred * lax.rsqrt(var + 1e-05) * gain


def double_gelu(x):
    inner = x * (0.7978845608028654 + (0.7978845608028654 * 0.044715) * (x * x))
    return x + x * jnp.tanh(inner)


def attend(tokens, gain, w_qv_t, w_k, w_out):
    normed = norm_rows(tokens, gain).astype(BF16)
    qv = lax.dot_general(w_qv_t, normed, (((1,), (1,)), ((), ())), preferred_element_type=F32)
    scale = HEAD ** -0.5 * math.log2(math.e)
    q_t = (qv[:WIDTH] * scale).astype(BF16)
    v_t = qv[WIDTH:].astype(BF16)
    keys = jnp.dot(normed, w_k, preferred_element_type=F32).astype(BF16)
    low = lax.broadcasted_iota(jnp.int32, (HEAD, 128), 1) < 64
    zero_q = jnp.zeros((64, 128), BF16)
    zero_p = jnp.zeros((64, 128), BF16)
    none = jnp.zeros((HEAD, 128), BF16)
    outs = []
    for a in range(2):
        here = q_t[:, 128 * a : 128 * (a + 1)]
        over = jnp.concatenate([here[:, 64:], here[:, :64]], axis=1)
        probs = []
        inverse = []
        for g in range(2):
            straight, crossed = (here, over) if g == 0 else (over, here)
            row0 = 128 * a + 64 * g
            for t in range(2):
                pair = []
                for jj in range(2):
                    at = 128 * t + 64 * jj
                    first = jnp.where(low, straight[at : at + HEAD], none)
                    second = jnp.where(low, none, crossed[at + HEAD : at + 64])
                    pair.append(jnp.concatenate([first, second], axis=0))
                rhs = jnp.concatenate(
                    [
                        jnp.concatenate([pair[0], zero_q], axis=1),
                        jnp.concatenate([zero_q, pair[1]], axis=1),
                    ],
                    axis=0,
                )
                scores = jnp.dot(
                    keys[row0 : row0 + 64, 128 * t : 128 * (t + 1)], rhs, preferred_element_type=F32
                )
                top = jnp.max(scores, axis=0, keepdims=True)
                weights = jnp.exp2(scores - top)
                total = jnp.sum(weights, axis=0, keepdims=True)
                probs.append(weights.astype(BF16))
                inverse.append(1.0 / total)
        for j in range(4):
            t, jj = j // 2, j % 2
            lanes = slice(128 * jj, 128 * (jj + 1))
            p0, p1 = probs[t][:, lanes], probs[2 + t][:, lanes]
            rhs = jnp.concatenate(
                [jnp.concatenate([p0, zero_p], axis=1), jnp.concatenate([zero_p, p1], axis=1)], axis=0
            )
            out = jnp.dot(
                v_t[64 * j : 64 * (j + 1), 128 * a : 128 * (a + 1)], rhs, preferred_element_type=F32
            )
            o0 = out[:, :128] * inverse[t][:, lanes]
            o1 = out[:, 128:] * inverse[2 + t][:, lanes]
            r0 = pltpu.roll(o0[HEAD:], 64, 1)
            r1 = pltpu.roll(o1[:HEAD], 64, 1)
            outs.append((a, jnp.where(low, o0[:HEAD], r1).astype(BF16)))
            outs.append((a, jnp.where(low, r0, o1[HEAD:]).astype(BF16)))
    mixed_t = jnp.concatenate(
        [jnp.concatenate([o for a, o in outs if a == half], axis=0) for half in range(2)], axis=1
    )
    added = lax.dot_general(mixed_t, w_out, (((0,), (0,)), ((), ())), preferred_element_type=F32)
    return tokens + added


def local_kernel(
    part,
    flags_ref,
    main_ref,
    above_ref,
    below_ref,
    north_ref,
    south_ref,
    side_ref,
    gain_ref,
    w_expand_ref,
    b_expand_ref,
    depth_ref,
    b_depth_ref,
    w_project_ref,
    gain2_ref,
    w_qv_ref,
    w_k_ref,
    w_out_ref,
    out_ref,
):
    per = 8 // PARTS
    band = pl.program_id(0) * 8 + part * per + pl.program_id(1)
    is_first = band == 0
    is_last = band == 15
    own = main_ref[...].astype(F32)
    top = jnp.where(is_first, north_ref[...].astype(F32), above_ref[...].astype(F32))
    bottom = jnp.where(is_last, south_ref[...].astype(F32), below_ref[...].astype(F32))
    top_keep = jnp.where(is_first, flags_ref[0], 1.0)
    bottom_keep = jnp.where(is_last, flags_ref[1], 1.0)
    left_keep, right_keep = flags_ref[2], flags_ref[3]
    cells = jnp.concatenate(
        [
            top.reshape(COLS, WIDTH),
            own.reshape(8 * COLS, WIDTH),
            bottom.reshape(COLS, WIDTH),
            side_ref[0].astype(F32),
        ],
        axis=0,
    )
    normed = norm_rows(cells, gain_ref[...]).astype(BF16)
    col = lax.broadcasted_iota(jnp.int32, (COLS, SLICE), 0)
    at_left = col == 0
    at_right = col == COLS - 1
    side_row = lax.broadcasted_iota(jnp.int32, (16, SLICE), 0)
    side_edge = jnp.where(side_row == 0, top_keep, jnp.where(side_row == 9, bottom_keep, 1.0))
    acc = own.reshape(8 * COLS, WIDTH)
    for s in range(WIDE // SLICE):
        lanes = slice(s * SLICE, (s + 1) * SLICE)
        grown = jnp.dot(normed, w_expand_ref[:, lanes], preferred_element_type=F32)
        grown = double_gelu(grown + b_expand_ref[:, lanes])
        rows = [grown[COLS * i : COLS * (i + 1)] for i in range(10)]
        rows[0] = rows[0] * top_keep
        rows[9] = rows[9] * bottom_keep
        rows = [r.astype(BF16).astype(F32) for r in rows]
        left = (grown[10 * COLS : 10 * COLS + 16] * (side_edge * left_keep)).astype(BF16).astype(F32)
        right = (grown[10 * COLS + 16 :] * (side_edge * right_keep)).astype(BF16).astype(F32)
        taps = [[depth_ref[3 * di + dj : 3 * di + dj + 1, lanes] for dj in range(3)] for di in range(3)]
        left = sum(taps[di][0] * left[di : di + 8] for di in range(3))
        right = sum(taps[di][2] * right[di : di + 8] for di in range(3))
        pieces = []
        for r in range(8):
            p = [
                taps[0][dj] * rows[r] + taps[1][dj] * rows[r + 1] + taps[2][dj] * rows[r + 2]
                for dj in range(3)
            ]
            from_left = jnp.where(at_left, left[r : r + 1], pltpu.roll(p[0], 1, 0))
            from_right = jnp.where(at_right, right[r : r + 1], pltpu.roll(p[2], COLS - 1, 0))
            total = (p[1] + b_depth_ref[:, lanes]) + (from_left + from_right)
            pieces.append(double_gelu(total).astype(BF16))
        filtered = jnp.concatenate(pieces, axis=0)
        acc = acc + jnp.dot(filtered, w_project_ref[lanes, :], preferred_element_type=F32)
    mixed = acc.astype(BF16).astype(F32)
    tokens = jnp.concatenate(
        [
            mixed[COLS * r + 8 * b : COLS * r + 8 * b + 8]
            for b in range(4)
            for r in range(8)
        ],
        axis=0,
    )
    done = attend(tokens, gain2_ref[...], w_qv_ref[...], w_k_ref[...], w_out_ref[...])
    done = jnp.concatenate(
        [done[64 * b + 8 * r : 64 * b + 8 * r + 8] for r in range(8) for b in range(4)], axis=0
    )
    out_ref[...] = done.astype(BF16).reshape(8, 1, COLS, WIDTH)


def local_stage(part, flags, field, north, south, side, weights):
    per = 8 // PARTS
    band = lambda i, r: i * 8 + part * per + r
    whole = lambda a: pl.BlockSpec(a.shape, lambda i, r: (0,) * a.ndim)
    return pl.pallas_call(
        functools.partial(local_kernel, part),
        grid=(2, per),
        in_specs=[
            pl.BlockSpec(memory_space=pltpu.SMEM),
            pl.BlockSpec((8, COLS, WIDTH), lambda i, r: (band(i, r), 0, 0)),
            pl.BlockSpec((1, COLS, WIDTH), lambda i, r: (jnp.maximum(band(i, r) * 8 - 1, 0), 0, 0)),
            pl.BlockSpec((1, COLS, WIDTH), lambda i, r: (jnp.minimum(band(i, r) * 8 + 8, 127), 0, 0)),
            whole(north),
            whole(south),
            pl.BlockSpec((1, COLS, WIDTH), lambda i, r: (band(i, r), 0, 0)),
        ]
        + [whole(w) for w in weights],
        out_specs=pl.BlockSpec((8, 1, COLS, WIDTH), lambda i, r: (r, i, 0, 0)),
        out_shape=jax.ShapeDtypeStruct((8 * per, 2, COLS, WIDTH), BF16),
        compiler_params=pltpu.CompilerParams(
            dimension_semantics=("arbitrary", "arbitrary"), vmem_limit_bytes=VMEM_LIMIT
        ),
        cost_estimate=pl.CostEstimate(
            flops=10_000_000_000 // PARTS, bytes_accessed=6_000_000 // PARTS, transcendentals=12_000_000 // PARTS
        ),
        name="local_stage",
    )(flags, field, field, field, north, south, side, *weights)


def grid_kernel(in_ref, gain_ref, w_qv_ref, w_k_ref, w_out_ref, out_ref):
    i = lax.broadcasted_iota(jnp.int32, (256, 256), 0)
    j = lax.broadcasted_iota(jnp.int32, (256, 256), 1)
    swap = jnp.where((i % 16) * 16 + i // 16 == j, 1.0, 0.0).astype(BF16)
    turned = []
    for c in range(4):
        block = in_ref[8 * c : 8 * c + 8].reshape(256, WIDTH)
        turned.append(jnp.dot(swap, block, preferred_element_type=F32))
    done = []
    for g in range(4):
        tokens = jnp.concatenate(
            [turned[c][64 * g + 16 * k : 64 * g + 16 * k + 16] for k in range(4) for c in range(4)], axis=0
        )
        done.append(
            attend(tokens, gain_ref[...], w_qv_ref[...], w_k_ref[...], w_out_ref[...]).astype(BF16)
        )
    for c in range(4):
        block = jnp.concatenate(
            [done[g][64 * k + 16 * c : 64 * k + 16 * c + 16] for g in range(4) for k in range(4)], axis=0
        )
        back = jnp.dot(swap, block, preferred_element_type=F32).astype(BF16)
        out_ref[8 * c : 8 * c + 8] = back.reshape(8, 1, 2, 16, WIDTH)


def grid_stage(landed, weights):
    rows = landed.shape[1]
    whole = lambda a: pl.BlockSpec(a.shape, lambda r, h: (0,) * a.ndim)
    block = pl.BlockSpec((32, 1, 2, 16, WIDTH), lambda r, h: (0, r, 0, h, 0))
    return pl.pallas_call(
        grid_kernel,
        grid=(rows, 2),
        in_specs=[block] + [whole(w) for w in weights],
        out_specs=block,
        out_shape=jax.ShapeDtypeStruct(landed.shape, BF16),
        compiler_params=pltpu.CompilerParams(
            dimension_semantics=("arbitrary", "arbitrary"), vmem_limit_bytes=VMEM_LIMIT
        ),
        cost_estimate=pl.CostEstimate(
            flops=6_000_000_000 // PARTS, bytes_accessed=5_000_000 // PARTS, transcendentals=2_000_000 // PARTS
        ),
        name="grid_stage",
    )(landed, *weights)


def shift(values, axis, step, count):
    pairs = [(i, i + step) for i in range(count) if 0 <= i + step < count]
    return lax.ppermute(values, axis, pairs)


LON = ("j", "m")


def per_device(
    field,
    norm_gain,
    expand_weight,
    expand_bias,
    depth_kernel,
    depth_bias,
    project_weight,
    block_gain,
    block_qkv,
    block_out,
    grid_gain,
    grid_qkv,
    grid_out,
):
    lat_count, lon_count = 4, 32
    north = shift(field[-1:], "lat", 1, lat_count)
    south = shift(field[:1], "lat", -1, lat_count)

    def side(at):
        return jnp.concatenate([north[:, at], field[:, at], south[:, at]], axis=0)

    left = shift(side(COLS - 1), LON, 1, lon_count)
    right = shift(side(0), LON, -1, lon_count)

    def windows(column):
        column = jnp.pad(column, ((0, 6), (0, 0))).reshape(17, 8, WIDTH)
        return jnp.concatenate([column[:16], column[1:]], axis=1)

    sides = jnp.concatenate([windows(left), windows(right)], axis=1)
    lat = lax.axis_index("lat")
    lon = lax.axis_index(LON)
    flags = jnp.stack([lat > 0, lat < lat_count - 1, lon > 0, lon < lon_count - 1]).astype(F32)

    def attend_weights(gain, qkv, out):
        q, k, v = qkv[:, :WIDTH], qkv[:, WIDTH : 2 * WIDTH], qkv[:, 2 * WIDTH :]
        return (gain[None], jnp.concatenate([q, v], axis=1).T, k, out)

    local_weights = (
        norm_gain[None],
        expand_weight,
        expand_bias[None],
        0.5 * depth_kernel.reshape(9, WIDE),
        depth_bias[None],
        (0.5 * project_weight.astype(F32)).astype(BF16),
    ) + attend_weights(block_gain, block_qkv, block_out)
    grid_weights = attend_weights(grid_gain, grid_qkv, grid_out)
    per_dest = 2 // PARTS
    landed = []
    for part in range(PARTS):
        parcels = local_stage(part, flags, field, north, south, sides, local_weights)
        parcels = parcels.reshape(32, per_dest * 2 * COLS, WIDTH)
        landed.append(lax.all_to_all(parcels, ("lat", "j"), 0, 0, tiled=True))
    results = []
    for part in range(PARTS):
        groups = landed[part].reshape(32, per_dest, 2, COLS, WIDTH)
        groups = grid_stage(groups, grid_weights)
        back = lax.all_to_all(groups.reshape(32, per_dest * 2 * COLS, WIDTH), ("lat", "j"), 0, 0, tiled=True)
        results.append(back.reshape(64 // PARTS, 2, COLS, WIDTH).transpose(1, 0, 2, 3))
    return jnp.concatenate(results, axis=1).reshape(128, COLS, WIDTH)


def solution(mesh):
    inner = Mesh(mesh.devices.reshape(4, 8, 4), ("lat", "j", "m"))
    return jax.shard_map(
        per_device,
        mesh=inner,
        in_specs=(P("lat", LON, None),) + (P(),) * 12,
        out_specs=P("lat", LON, None),
        check_vma=False,
    )
```

profile of v0, /device:TPU:1, one launch (start us, length us, event | category | flops | bytes accessed | tf_op | source)
XLA Modules:
  0.0 173.4 jit_solution(7000081908418285383)
XLA Ops:
  0.0 0.0 copy-start.2
  0.0 0.8 fusion.3
  0.8 3.3 %collective-permute-start.1 = (bf16[1,32,256]{2,1,0:T(8,128)(2,1)S(1)}, bf16[1,32,256]{2,1,0:T(8,128)(2,1)S(1)}, u32[]{:S(2)}, u32[]{:S(2)}) collective-permute-start(bf16[1,32,256]{2,1,0:T(8,128)(2,1)S(1)} %get-tuple-element.7), channel_id=1, source_target_pairs={{32,0},{64,32},{96,64},{33,1},{65,33},{97,65},{34,2},{66,34},{98,6... | collective-permute-start | bytes 49160 | tf_op jit(solution)/shard_map/ppermute | solution.py:264
  4.1 3.5 %collective-permute-start = (bf16[1,32,256]{2,1,0:T(8,128)(2,1)S(1)}, bf16[1,32,256]{2,1,0:T(8,128)(2,1)S(1)}, u32[]{:S(2)}, u32[]{:S(2)}) collective-permute-start(bf16[1,32,256]{2,1,0:T(8,128)(2,1)S(1)} %get-tuple-element.8), channel_id=1, source_target_pairs={{0,32},{32,64},{64,96},{1,33},{33,65},{65,97},{2,34},{34,66},{66,9... | collective-permute-start | bytes 49160 | tf_op jit(solution)/shard_map/ppermute | solution.py:264
  7.7 1.4 fusion.2
  9.1 0.8 broadcast_multiply_fusion
  9.9 1.7 fusion.5
  11.6 0.1 copy.30
  11.7 0.1 copy.31
  11.9 0.0 copy-done.2
  11.9 0.9 multiply_convert_fusion.w_project_ref
  12.8 0.7 maximum_bitcast_fusion.w_qv_ref
  13.5 0.7 add_convert_fusion.flags_ref
  14.1 0.6 mul.20.depth_ref
  14.8 0.0 collective-permute-done.1.south_ref
  14.8 0.0 copy-start.4
  14.8 0.0 collective-permute-done.north_ref
  14.8 0.0 copy-start.5
  14.9 1.3 collective-permute-start.3
  16.2 5.8 %collective-permute-start.2 = (bf16[130,256]{1,0:T(8,128)(2,1)S(1)}, bf16[130,256]{1,0:T(8,128)(2,1)S(1)}, u32[]{:S(2)}, u32[]{:S(2)}) collective-permute-start(bf16[130,256]{1,0:T(8,128)(2,1)S(1)} %pad_maximum_fusion.2), channel_id=1, source_target_pairs={{0,1},{1,2},{2,3},{3,4},{4,5},{5,6},{6,7},{7,8},{8,9},{9,10},{10,1... | collective-permute-start | bytes 199688 | tf_op jit(solution)/shard_map/ppermute | solution.py:264
  22.1 0.0 collective-permute-done.3
  22.1 2.1 %collective-permute-done.2 = bf16[130,256]{1,0:T(8,128)(2,1)S(1)} collective-permute-done((bf16[130,256]{1,0:T(8,128)(2,1)S(1)}, bf16[130,256]{1,0:T(8,128)(2,1)S(1)}, u32[]{:S(2)}, u32[]{:S(2)}) %collective-permute-start.2) | collective-permute-done | bytes 66592 | tf_op jit(solution)/shard_map/ppermute | solution.py:264
  24.2 0.7 pad_maximum_fusion.1.side_ref
  25.0 0.0 copy-done.4
  25.0 0.0 copy-done.5
  25.0 30.8 %local_stage.3 = bf16[32,2,32,256]{3,2,1,0:T(8,128)(2,1)} custom-call(f32[4]{0:T(128)} %add_convert_fusion.flags_ref, bf16[128,32,256]{2,1,0:T(8,128)(2,1)} %below_ref.3, bf16[128,32,256]{2,1,0:T(8,128)(2,1)} %below_ref.3, bf16[128,32,256]{2,1,0:T(8,128)(2,1)} %below_ref.3, bf16[1,32,256]{2,1,0:T(8,128)(2,1)} %copy-done.5, bf16[1,32,256]{2,1,0:T(8,128)(2,1)} %copy-done.4, ...), custom_call_target="tpu_custom_call" | custom-call | flops 5000000000 | bytes 3000000 | tf_op jit(solution)/shard_map/local_stage/pallas_call | solution.py:193
  55.8 13.8 %all-to-all-start.2 = ((bf16[32,64,256]{2,1,0:T(8,128)(2,1)}), bf16[32,64,256]{2,1,0:T(8,128)(2,1)S(1)}, u32[]{:S(2)}, u32[]{:S(2)}) async-start(bf16[32,64,256]{2,1,0:T(8,128)(2,1)} %bitcast.59), calls=%async_computation.2 | async-start | bytes 2097152 | tf_op jit(solution)/shard_map/all_to_all | solution.py:322
  69.6 30.8 %local_stage.2 = bf16[32,2,32,256]{3,2,1,0:T(8,128)(2,1)} custom-call(f32[4]{0:T(128)} %add_convert_fusion.flags_ref, bf16[128,32,256]{2,1,0:T(8,128)(2,1)} %below_ref.3, bf16[128,32,256]{2,1,0:T(8,128)(2,1)} %below_ref.3, bf16[128,32,256]{2,1,0:T(8,128)(2,1)} %below_ref.3, bf16[1,32,256]{2,1,0:T(8,128)(2,1)} %copy-done.5, bf16[1,32,256]{2,1,0:T(8,128)(2,1)} %copy-done.4, ...), custom_call_target="tpu_custom_call" | custom-call | flops 5000000000 | bytes 3000000 | tf_op jit(solution)/shard_map/local_stage/pallas_call | solution.py:193
  100.4 0.0 copy-start.3
  100.4 0.0 all-to-all-done.2
  100.4 0.0 copy-start
  100.4 8.4 %all-to-all-start = ((bf16[32,64,256]{2,1,0:T(8,128)(2,1)}), bf16[32,64,256]{2,1,0:T(8,128)(2,1)S(1)}, u32[]{:S(2)}, u32[]{:S(2)}) async-start(bf16[32,64,256]{2,1,0:T(8,128)(2,1)} %bitcast.55), calls=%async_computation | async-start | bytes 2097152 | tf_op jit(solution)/shard_map/all_to_all | solution.py:322
  108.8 0.0 copy-done.3
  108.9 0.7 fusion.4
  109.5 0.1 copy.32
  109.6 0.1 copy.33
  109.8 0.7 maximum_bitcast_fusion.1.w_qv_ref
  110.5 0.0 copy-done
  110.5 11.1 %grid_stage.3 = bf16[32,1,2,32,256]{4,3,2,1,0:T(8,128)(2,1)} custom-call(bf16[32,1,2,32,256]{4,3,2,1,0:T(8,128)(2,1)} %bitcast.54, f32[1,256]{1,0:T(1,128)} %bitcast.70, bf16[512,256]{1,0:T(8,128)(2,1)} %maximum_bitcast_fusion.1.w_qv_ref, bf16[256,256]{1,0:T(8,128)(2,1)} %get-tuple-element.9.w_k_ref, bf16[256,256]{1,0:T(8,128)(2,1)} %w_out_ref.7), custom_call_target="tpu_custom_call" | custom-call | flops 3000000000 | bytes 2500000 | tf_op jit(solution)/shard_map/grid_stage/pallas_call | solution.py:246
  121.6 5.1 %all-to-all-done = bf16[32,64,256]{2,1,0:T(8,128)(2,1)S(1)} async-done(((bf16[32,64,256]{2,1,0:T(8,128)(2,1)}), bf16[32,64,256]{2,1,0:T(8,128)(2,1)S(1)}, u32[]{:S(2)}, u32[]{:S(2)}) %all-to-all-start) | async-done | bytes 1048608 | tf_op jit(solution)/shard_map/all_to_all | solution.py:322
  126.7 0.0 copy-start.1
  126.7 4.7 %all-to-all-start.3 = ((bf16[32,64,256]{2,1,0:T(8,128)(2,1)}), bf16[32,64,256]{2,1,0:T(8,128)(2,1)S(1)}, u32[]{:S(2)}, u32[]{:S(2)}) async-start(bf16[32,64,256]{2,1,0:T(8,128)(2,1)} %bitcast.57), calls=%async_computation.3 | async-start | bytes 2097152 | tf_op jit(solution)/shard_map/all_to_all | solution.py:327
  131.4 0.0 copy-done.1
  131.5 11.1 %grid_stage.2 = bf16[32,1,2,32,256]{4,3,2,1,0:T(8,128)(2,1)} custom-call(bf16[32,1,2,32,256]{4,3,2,1,0:T(8,128)(2,1)} %bitcast.56, f32[1,256]{1,0:T(1,128)} %bitcast.71, bf16[512,256]{1,0:T(8,128)(2,1)} %maximum_bitcast_fusion.1.w_qv_ref, bf16[256,256]{1,0:T(8,128)(2,1)} %get-tuple-element.9.w_k_ref, bf16[256,256]{1,0:T(8,128)(2,1)} %w_out_ref.7), custom_call_target="tpu_custom_call" | custom-call | flops 3000000000 | bytes 2500000 | tf_op jit(solution)/shard_map/grid_stage/pallas_call | solution.py:246
  142.6 6.8 %all-to-all-done.3 = bf16[32,64,256]{2,1,0:T(8,128)(2,1)S(1)} async-done(((bf16[32,64,256]{2,1,0:T(8,128)(2,1)}), bf16[32,64,256]{2,1,0:T(8,128)(2,1)S(1)}, u32[]{:S(2)}, u32[]{:S(2)}) %all-to-all-start.3) | async-done | bytes 1048608 | tf_op jit(solution)/shard_map/all_to_all | solution.py:327
  149.3 4.6 %all-to-all-start.1 = ((bf16[32,64,256]{2,1,0:T(8,128)(2,1)}), bf16[32,64,256]{2,1,0:T(8,128)(2,1)S(1)}, u32[]{:S(2)}, u32[]{:S(2)}) async-start(bf16[32,64,256]{2,1,0:T(8,128)(2,1)} %bitcast.58), calls=%async_computation.1 | async-start | bytes 2097152 | tf_op jit(solution)/shard_map/all_to_all | solution.py:327
  153.9 0.1 copy.38
  154.0 17.8 %all-to-all-done.1 = bf16[32,64,256]{2,1,0:T(8,128)(2,1)S(1)} async-done(((bf16[32,64,256]{2,1,0:T(8,128)(2,1)}), bf16[32,64,256]{2,1,0:T(8,128)(2,1)S(1)}, u32[]{:S(2)}, u32[]{:S(2)}) %all-to-all-start.1) | async-done | bytes 1048608 | tf_op jit(solution)/shard_map/all_to_all | solution.py:327
  171.8 0.1 copy.39
  171.9 1.5 pad_maximum_fusion
  (8 shorter events, 0.1 us)
Async XLA Ops:
  0.0 11.9 %copy-start.2 = (bf16[1024,256]{1,0:T(8,128)(2,1)S(1)}, bf16[1024,256]{1,0:T(8,128)(2,1)}, u32[]{:S(2)}) copy-start(bf16[1024,256]{1,0:T(8,128)(2,1)} %param.19) | copy-start | bytes 1572868
  0.8 14.0 %collective-permute-start.1 = (bf16[1,32,256]{2,1,0:T(8,128)(2,1)S(1)}, bf16[1,32,256]{2,1,0:T(8,128)(2,1)S(1)}, u32[]{:S(2)}, u32[]{:S(2)}) collective-permute-start(bf16[1,32,256]{2,1,0:T(8,128)(2,1)S(1)} %get-tuple-element.7), channel_id=1, source_target_pairs={{32,0},{64,32},{96,64},{33,1},{65,33},{97,65},{34,2},{66,34},{98,6... | collective-permute-start | bytes 49160 | tf_op jit(solution)/shard_map/ppermute | solution.py:264
  4.1 10.7 %collective-permute-start = (bf16[1,32,256]{2,1,0:T(8,128)(2,1)S(1)}, bf16[1,32,256]{2,1,0:T(8,128)(2,1)S(1)}, u32[]{:S(2)}, u32[]{:S(2)}) collective-permute-start(bf16[1,32,256]{2,1,0:T(8,128)(2,1)S(1)} %get-tuple-element.8), channel_id=1, source_target_pairs={{0,32},{32,64},{64,96},{1,33},{33,65},{65,97},{2,34},{34,66},{66,9... | collective-permute-start | bytes 49160 | tf_op jit(solution)/shard_map/ppermute | solution.py:264
  14.8 10.2 %copy-start.4 = (bf16[1,32,256]{2,1,0:T(8,128)(2,1)}, bf16[1,32,256]{2,1,0:T(8,128)(2,1)S(1)}, u32[]{:S(2)}) copy-start(bf16[1,32,256]{2,1,0:T(8,128)(2,1)S(1)} %collective-permute-done.1.south_ref) | copy-start | bytes 49156
  14.8 10.1 %copy-start.5 = (bf16[1,32,256]{2,1,0:T(8,128)(2,1)}, bf16[1,32,256]{2,1,0:T(8,128)(2,1)S(1)}, u32[]{:S(2)}) copy-start(bf16[1,32,256]{2,1,0:T(8,128)(2,1)S(1)} %collective-permute-done.north_ref) | copy-start | bytes 49156
  14.9 7.2 %collective-permute-start.3 = (bf16[130,256]{1,0:T(8,128)(2,1)S(1)}, bf16[130,256]{1,0:T(8,128)(2,1)S(1)}, u32[]{:S(2)}, u32[]{:S(2)}) collective-permute-start(bf16[130,256]{1,0:T(8,128)(2,1)S(1)} %pad_maximum_fusion.3), channel_id=1, source_target_pairs={{1,0},{2,1},{3,2},{4,3},{5,4},{6,5},{7,6},{8,7},{9,8},{10,9},{11,1... | collective-permute-start | bytes 199688 | tf_op jit(solution)/shard_map/ppermute | solution.py:264
  16.2 8.0 %collective-permute-start.2 = (bf16[130,256]{1,0:T(8,128)(2,1)S(1)}, bf16[130,256]{1,0:T(8,128)(2,1)S(1)}, u32[]{:S(2)}, u32[]{:S(2)}) collective-permute-start(bf16[130,256]{1,0:T(8,128)(2,1)S(1)} %pad_maximum_fusion.2), channel_id=1, source_target_pairs={{0,1},{1,2},{2,3},{3,4},{4,5},{5,6},{6,7},{7,8},{8,9},{9,10},{10,1... | collective-permute-start | bytes 199688 | tf_op jit(solution)/shard_map/ppermute | solution.py:264
  55.8 44.6 %all-to-all-start.2 = ((bf16[32,64,256]{2,1,0:T(8,128)(2,1)}), bf16[32,64,256]{2,1,0:T(8,128)(2,1)S(1)}, u32[]{:S(2)}, u32[]{:S(2)}) async-start(bf16[32,64,256]{2,1,0:T(8,128)(2,1)} %bitcast.59), calls=%async_computation.2 | async-start | bytes 2097152 | tf_op jit(solution)/shard_map/all_to_all | solution.py:322
  100.4 8.5 %copy-start.3 = (bf16[256,768]{1,0:T(8,128)(2,1)S(1)}, bf16[256,768]{1,0:T(8,128)(2,1)}, u32[]{:S(2)}) copy-start(bf16[256,768]{1,0:T(8,128)(2,1)} %param.24) | copy-start | bytes 1179652
  100.4 10.1 %copy-start = (bf16[32,64,256]{2,1,0:T(8,128)(2,1)}, bf16[32,64,256]{2,1,0:T(8,128)(2,1)S(1)}, u32[]{:S(2)}) copy-start(bf16[32,64,256]{2,1,0:T(8,128)(2,1)S(1)} %all-to-all-done.2) | copy-start | bytes 3145732
  100.4 26.3 %all-to-all-start = ((bf16[32,64,256]{2,1,0:T(8,128)(2,1)}), bf16[32,64,256]{2,1,0:T(8,128)(2,1)S(1)}, u32[]{:S(2)}, u32[]{:S(2)}) async-start(bf16[32,64,256]{2,1,0:T(8,128)(2,1)} %bitcast.55), calls=%async_computation | async-start | bytes 2097152 | tf_op jit(solution)/shard_map/all_to_all | solution.py:322
  126.7 4.7 %copy-start.1 = (bf16[32,64,256]{2,1,0:T(8,128)(2,1)}, bf16[32,64,256]{2,1,0:T(8,128)(2,1)S(1)}, u32[]{:S(2)}) copy-start(bf16[32,64,256]{2,1,0:T(8,128)(2,1)S(1)} %all-to-all-done) | copy-start | bytes 3145732
  126.7 22.6 %all-to-all-start.3 = ((bf16[32,64,256]{2,1,0:T(8,128)(2,1)}), bf16[32,64,256]{2,1,0:T(8,128)(2,1)S(1)}, u32[]{:S(2)}, u32[]{:S(2)}) async-start(bf16[32,64,256]{2,1,0:T(8,128)(2,1)} %bitcast.57), calls=%async_computation.3 | async-start | bytes 2097152 | tf_op jit(solution)/shard_map/all_to_all | solution.py:327
  149.3 22.5 %all-to-all-start.1 = ((bf16[32,64,256]{2,1,0:T(8,128)(2,1)}), bf16[32,64,256]{2,1,0:T(8,128)(2,1)S(1)}, u32[]{:S(2)}, u32[]{:S(2)}) async-start(bf16[32,64,256]{2,1,0:T(8,128)(2,1)} %bitcast.58), calls=%async_computation.1 | async-start | bytes 2097152 | tf_op jit(solution)/shard_map/all_to_all | solution.py:327
where the time goes:
time: 174 us; the launch traced here: 173 us
  Pallas kernels  83.8 us (48%)
  starting transfers between devices  45.6 us (26%)
  waiting for transfers between devices  31.9 us (18%)
  other arithmetic  6.09 us (4%)
  local copies, waits for them, and re-layouts  5.88 us (3%)
    pallas_call x2, Pallas kernels, local_stage(): pl.pallas_call(functools.partial(local_kernel, part), grid=(2, per), in_s...  61.5 us
    all_to_all x2, waiting for transfers between devices, per_device(): lax.all_to_all(groups.reshape(32, per_dest * 2 * COLS, WIDTH), ('lat', 'j...  24.6 us
    all_to_all x2, starting transfers between devices, per_device(): landed.append(lax.all_to_all(parcels, ('lat', 'j'), 0, 0, tiled=True))  22.3 us
    pallas_call x2, Pallas kernels, grid_stage(): pl.pallas_call(grid_kernel, grid=(rows, 2), in_specs=[block] + [whole(w)...  22.2 us
    ppermute x4, starting transfers between devices, shift(): return lax.ppermute(values, axis, pairs)  14 us
    all_to_all x2, starting transfers between devices, per_device(): lax.all_to_all(groups.reshape(32, per_dest * 2 * COLS, WIDTH), ('lat', 'j...  9.31 us
    all_to_all x2, waiting for transfers between devices, per_device(): landed.append(lax.all_to_all(parcels, ('lat', 'j'), 0, 0, tiled=True))  5.13 us
  transfers between devices with their start and end apart: 8, of which 4 were waited for; matrix products, arithmetic and copies ran while one was open for 5% of the time, Pallas kernels for 31%

commit v1 on v0

v1 whole, which is shorter than its diff:
```python
import functools
import math

import jax
import jax.numpy as jnp
from jax import lax
from jax.experimental import pallas as pl
from jax.experimental.pallas import tpu as pltpu
from jax.sharding import Mesh
from jax.sharding import PartitionSpec as P

HEADS = 8
WIDTH = 256
HEAD = WIDTH // HEADS
WIDE = 1024
COLS = 32
SLICE = 256
F32 = jnp.float32
BF16 = jnp.bfloat16
VMEM_LIMIT = 56 * 1024 * 1024


def norm_rows(values, gain):
    mean = jnp.mean(values, axis=-1, keepdims=True)
    centred = values - mean
    var = jnp.mean(centred * centred, axis=-1, keepdims=True)
    return centred * lax.rsqrt(var + 1e-05) * gain


def double_gelu(x):
    c0 = jnp.asarray(0.7978845608028654, x.dtype)
    c1 = jnp.asarray(0.7978845608028654 * 0.044715, x.dtype)
    return x + x * jnp.tanh(x * (c0 + c1 * (x * x)))


def swap_matrix():
    i = lax.broadcasted_iota(jnp.int32, (256, 256), 0)
    j = lax.broadcasted_iota(jnp.int32, (256, 256), 1)
    return jnp.where((i % 16) * 16 + i // 16 == j, 1.0, 0.0).astype(BF16)


def attend(tokens, gain, w_qkv, w_out):
    count = tokens.shape[0]
    normed = norm_rows(tokens, gain).astype(BF16)
    scale = HEAD ** -0.5 * math.log2(math.e)
    w_qv_t = jnp.concatenate([w_qkv[:, :WIDTH], w_qkv[:, 2 * WIDTH :]], axis=1).T
    keys = jnp.dot(normed, w_qkv[:, WIDTH : 2 * WIDTH], preferred_element_type=F32).astype(BF16)
    low = lax.broadcasted_iota(jnp.int32, (HEAD, 128), 1) < 64
    zero = jnp.zeros((64, 128), BF16)
    none = jnp.zeros((HEAD, 128), BF16)
    q_t, v_t = [], []
    for i in range(count // 256):
        qv = lax.dot_general(
            w_qv_t,
            normed[256 * i : 256 * (i + 1)],
            (((1,), (1,)), ((), ())),
            preferred_element_type=F32,
        )
        q_t += [(qv[:WIDTH, 128 * a : 128 * (a + 1)] * scale).astype(BF16) for a in range(2)]
        v_t += [qv[WIDTH:, 128 * a : 128 * (a + 1)].astype(BF16) for a in range(2)]
    scores = {}
    for n, here in enumerate(q_t):
        over = jnp.concatenate([here[:, 64:], here[:, :64]], axis=1)
        for g in range(2):
            straight, crossed = (here, over) if g == 0 else (over, here)
            row0 = 128 * n + 64 * g
            for t in range(2):
                pair = []
                for jj in range(2):
                    at = 128 * t + 64 * jj
                    first = jnp.where(low, straight[at : at + HEAD], none)
                    second = jnp.where(low, none, crossed[at + HEAD : at + 64])
                    pair.append(jnp.concatenate([first, second], axis=0))
                rhs = jnp.concatenate(
                    [
                        jnp.concatenate([pair[0], zero], axis=1),
                        jnp.concatenate([zero, pair[1]], axis=1),
                    ],
                    axis=0,
                )
                scores[n, g, t] = jnp.dot(
                    keys[row0 : row0 + 64, 128 * t : 128 * (t + 1)], rhs, preferred_element_type=F32
                )
    probs, inverse = {}, {}
    for at, score in scores.items():
        weights = jnp.exp2(score - jnp.max(score, axis=0, keepdims=True))
        inverse[at] = 1.0 / jnp.sum(weights, axis=0, keepdims=True)
        probs[at] = weights.astype(BF16)
    raw = {}
    for n in range(count // 128):
        for j in range(4):
            t, jj = j // 2, j % 2
            lanes = slice(128 * jj, 128 * (jj + 1))
            p0, p1 = probs[n, 0, t][:, lanes], probs[n, 1, t][:, lanes]
            rhs = jnp.concatenate(
                [jnp.concatenate([p0, zero], axis=1), jnp.concatenate([zero, p1], axis=1)], axis=0
            )
            raw[n, j] = jnp.dot(v_t[n][64 * j : 64 * (j + 1)], rhs, preferred_element_type=F32)
    mixed = []
    for n in range(count // 128):
        outs = []
        for j in range(4):
            t, jj = j // 2, j % 2
            lanes = slice(128 * jj, 128 * (jj + 1))
            o0 = raw[n, j][:, :128] * inverse[n, 0, t][:, lanes]
            o1 = raw[n, j][:, 128:] * inverse[n, 1, t][:, lanes]
            outs.append(jnp.where(low, o0[:HEAD], pltpu.roll(o1[:HEAD], 64, 1)).astype(BF16))
            outs.append(jnp.where(low, pltpu.roll(o0[HEAD:], 64, 1), o1[HEAD:]).astype(BF16))
        mixed.append(jnp.concatenate(outs, axis=0).T)
    mixed = jnp.concatenate(mixed, axis=0)
    return tokens + jnp.dot(mixed, w_out, preferred_element_type=F32)


def local_kernel(
    blocks,
    field_ref,
    north_ref,
    south_ref,
    *refs,
):
    edge = 0 in blocks
    if edge:
        side_ref, refs = refs[0], refs[1:]
    (
        gain_ref,
        w_expand_ref,
        b_expand_ref,
        depth_ref,
        b_depth_ref,
        w_project_ref,
        gain2_ref,
        w_qkv_ref,
        w_out_ref,
        out_ref,
        normed_ref,
        grown_ref,
        filtered_ref,
        acc_ref,
    ) = refs
    row = lax.broadcasted_iota(jnp.int32, (160, 512), 0)
    lane = lax.broadcasted_iota(jnp.int32, (160, 512), 1)
    same_band = row % 16 == lane // COLS
    col_gap = lane % COLS - row // 16
    k_of = lax.broadcasted_iota(jnp.int32, (160, SLICE), 0) % 16
    lat = lax.axis_index("lat")
    lon = lax.axis_index("j") * lax.axis_size("m") + lax.axis_index("m")
    keep_left = jnp.where(lon == 0, 0.0, 1.0)
    keep_right = jnp.where(lon == 8 * lax.axis_size("m") - 1, 0.0, 1.0)
    keep_top = jnp.where((k_of == 0) & (lat == 0), 0.0, 1.0).astype(BF16)
    keep_bottom = jnp.where((k_of == 15) & (lat == 3), 0.0, 1.0).astype(BF16)
    swap = swap_matrix()
    halves = []
    for block in blocks:
        window = 8 * block - 1
        pick = jnp.where(same_band & (col_gap == window), 1.0, 0.0).astype(BF16)
        on_side = block == 0 or block == COLS // 8 - 1
        if on_side:
            srow = lax.broadcasted_iota(jnp.int32, (160, 32), 0)
            slane = lax.broadcasted_iota(jnp.int32, (160, 32), 1)
            column = 0 if block == 0 else 9
            lane0 = 0 if block == 0 else 16
            pick_side = jnp.where(
                (srow // 16 == column) & (srow % 16 + lane0 == slane), 1.0, 0.0
            ).astype(BF16)
        for r in range(10):
            if r == 0:
                rows = jnp.concatenate(
                    [north_ref[...]] + [field_ref[8 * k + 7 : 8 * k + 8] for k in range(15)], axis=0
                )
            elif r == 9:
                rows = jnp.concatenate(
                    [field_ref[8 * k : 8 * k + 1] for k in range(1, 16)] + [south_ref[...]], axis=0
                )
            else:
                rows = jnp.concatenate(
                    [field_ref[8 * k + r - 1 : 8 * k + r] for k in range(16)], axis=0
                )
            cells = jnp.dot(pick, rows.reshape(512, WIDTH), preferred_element_type=F32)
            if on_side:
                cells = cells + jnp.dot(pick_side, side_ref[r], preferred_element_type=F32)
            if 1 <= r <= 8:
                acc_ref[128 * (r - 1) : 128 * r] = cells[16:144]
            normed_ref[160 * r : 160 * (r + 1)] = norm_rows(cells, gain_ref[...]).astype(BF16)

        def channels(s, _):
            at = pl.ds(pl.multiple_of(s * SLICE, SLICE), SLICE)
            bias = jnp.broadcast_to(b_expand_ref[:, at], (16, SLICE)).astype(BF16)
            bias = jnp.concatenate([bias] * 10, axis=0)
            w_here = w_expand_ref[:, at]
            grown = jnp.dot(normed_ref[...], w_here, preferred_element_type=F32).astype(BF16)
            for r in range(10):
                g = double_gelu(grown[160 * r : 160 * (r + 1)] + bias)
                if r == 0:
                    g = g * keep_top
                if r == 9:
                    g = g * keep_bottom
                if on_side:
                    keep = keep_left if block == 0 else keep_right
                    if block == 0:
                        g = jnp.concatenate([(g[:16] * keep.astype(BF16)), g[16:]], axis=0)
                    else:
                        g = jnp.concatenate([g[:144], (g[144:] * keep.astype(BF16))], axis=0)
                grown_ref[r] = g.reshape(10, 16, SLICE)
            for half in range(SLICE // 128):
                lanes = slice(128 * half, 128 * (half + 1))
                there = pl.ds(pl.multiple_of(s * SLICE + 128 * half, 128), 128)
                taps = [
                    jnp.broadcast_to(0.5 * depth_ref[i : i + 1, there], (16, 128)).astype(BF16)
                    for i in range(9)
                ]
                depth_bias = jnp.broadcast_to(b_depth_ref[:, there], (16, 128)).astype(BF16)
                for c in range(8):
                    near = [[grown_ref[r, c + dj, :, lanes] for r in range(10)] for dj in range(3)]
                    for r in range(8):
                        p = [
                            taps[dj] * near[dj][r]
                            + taps[3 + dj] * near[dj][r + 1]
                            + taps[6 + dj] * near[dj][r + 2]
                            for dj in range(3)
                        ]
                        total = (p[0] + p[1]) + (p[2] + depth_bias)
                        filtered_ref[r, c, :, lanes] = double_gelu(total)
            acc_ref[...] += jnp.dot(
                filtered_ref[...].reshape(1024, SLICE),
                w_project_ref[at, :] * jnp.asarray(0.5, BF16),
                preferred_element_type=F32,
            )
            return 0

        lax.fori_loop(0, WIDE // SLICE, channels, 0)
        mixed = acc_ref[...].astype(BF16)
        turned = [
            jnp.dot(swap, mixed[256 * i : 256 * (i + 1)], preferred_element_type=F32) for i in range(4)
        ]
        tokens = jnp.concatenate(
            [turned[i][16 * k : 16 * k + 16] for k in range(16) for i in range(4)], axis=0
        )
        halves.append(attend(tokens, gain2_ref[...], w_qkv_ref[...], w_out_ref[...]))
    for k in range(16):
        both = jnp.concatenate(
            [halves[h][64 * k : 64 * k + 64].reshape(8, 8, WIDTH) for h in range(2)], axis=1
        )
        out_ref[8 * (k % 8) : 8 * (k % 8) + 8, k // 8] = both.astype(BF16)


def local_stage(blocks, field, north, south, side, weights):
    vmem = pl.BlockSpec(memory_space=pltpu.VMEM)
    arrays = (field, north, south) + ((side,) if 0 in blocks else ()) + weights
    return pl.pallas_call(
        functools.partial(local_kernel, blocks),
        in_specs=[vmem] * len(arrays),
        out_specs=vmem,
        out_shape=jax.ShapeDtypeStruct((64, 2, 16, WIDTH), BF16),
        scratch_shapes=[
            pltpu.VMEM((1600, WIDTH), BF16),
            pltpu.VMEM((10, 10, 16, SLICE), BF16),
            pltpu.VMEM((8, 8, 16, SLICE), BF16),
            pltpu.VMEM((1024, WIDTH), F32),
        ],
        compiler_params=pltpu.CompilerParams(vmem_limit_bytes=VMEM_LIMIT),
        cost_estimate=pl.CostEstimate(
            flops=5_000_000_000, bytes_accessed=3_000_000, transcendentals=6_000_000
        ),
        name="local_stage",
    )(*arrays)


def grid_kernel(in_ref, gain_ref, w_qkv_ref, w_out_ref, out_ref):
    swap = swap_matrix()
    turned = []
    for c in range(4):
        block = in_ref[8 * c : 8 * c + 8].reshape(256, WIDTH)
        turned.append(jnp.dot(swap, block, preferred_element_type=F32))
    tokens = jnp.concatenate(
        [turned[c][16 * k : 16 * k + 16] for k in range(16) for c in range(4)], axis=0
    )
    done = attend(tokens, gain_ref[...], w_qkv_ref[...], w_out_ref[...]).astype(BF16)
    for c in range(4):
        block = jnp.concatenate([done[64 * k + 16 * c : 64 * k + 16 * c + 16] for k in range(16)], axis=0)
        back = jnp.dot(swap, block, preferred_element_type=F32).astype(BF16)
        out_ref[8 * c : 8 * c + 8] = back.reshape(8, 1, 2, 16, WIDTH)


def grid_stage(landed, weights):
    rows = landed.shape[1]
    whole = lambda a: pl.BlockSpec(a.shape, lambda r: (0,) * a.ndim)
    block = pl.BlockSpec((32, 1, 2, 16, WIDTH), lambda r: (0, r, 0, 0, 0))
    return pl.pallas_call(
        grid_kernel,
        grid=(rows,),
        in_specs=[block] + [whole(w) for w in weights],
        out_specs=block,
        out_shape=jax.ShapeDtypeStruct(landed.shape, BF16),
        compiler_params=pltpu.CompilerParams(
            dimension_semantics=("arbitrary",), vmem_limit_bytes=VMEM_LIMIT
        ),
        cost_estimate=pl.CostEstimate(
            flops=3_000_000_000, bytes_accessed=2_500_000, transcendentals=1_000_000
        ),
        name="grid_stage",
    )(landed, *weights)


def shift(values, axis, step, count):
    pairs = [(i, i + step) for i in range(count) if 0 <= i + step < count]
    return lax.ppermute(values, axis, pairs)


LON = ("j", "m")


def per_device(
    field,
    norm_gain,
    expand_weight,
    expand_bias,
    depth_kernel,
    depth_bias,
    project_weight,
    block_gain,
    block_qkv,
    block_out,
    grid_gain,
    grid_qkv,
    grid_out,
):
    lat_count, lon_count = 4, 32
    north = shift(field[-1:], "lat", 1, lat_count)
    south = shift(field[:1], "lat", -1, lat_count)

    def side(at):
        return jnp.concatenate([north[:, at], field[:, at], south[:, at]], axis=0)

    left = shift(side(COLS - 1), LON, 1, lon_count)
    right = shift(side(0), LON, -1, lon_count)

    def bands(column):
        middle = column[1:129].reshape(16, 8, WIDTH).transpose(1, 0, 2)
        first = jnp.concatenate([column[None, :1], middle[7:, :15]], axis=1)
        last = jnp.concatenate([middle[:1, 1:], column[None, 129:]], axis=1)
        return jnp.concatenate([first, middle, last], axis=0)

    sides = jnp.concatenate([bands(left), bands(right)], axis=1)
    local_weights = (
        norm_gain[None],
        expand_weight,
        expand_bias[None],
        depth_kernel.reshape(9, WIDE),
        depth_bias[None],
        project_weight,
        block_gain[None],
        block_qkv,
        block_out,
    )
    grid_weights = (grid_gain[None], grid_qkv, grid_out)
    shape = (32, 64, WIDTH)
    inner = local_stage((1, 2), field, north, south, None, local_weights)
    sides, inner = lax.optimization_barrier((sides, inner))
    outer = local_stage((0, 3), field, north, south, sides, local_weights)
    landed = [
        lax.all_to_all(parcels.reshape(shape), ("lat", "j"), 0, 0, tiled=True) for parcels in (inner, outer)
    ]
    results = []
    for groups in landed:
        groups = grid_stage(groups.reshape(32, 2, 2, 16, WIDTH), grid_weights)
        back = lax.all_to_all(groups.reshape(shape), ("lat", "j"), 0, 0, tiled=True)
        results.append(back.reshape(64, 2, 16, WIDTH))
    inner, outer = results
    whole = jnp.concatenate([outer[:, :, :8], inner, outer[:, :, 8:]], axis=2)
    return whole.transpose(1, 0, 2, 3).reshape(128, COLS, WIDTH)


def solution(mesh):
    inner = Mesh(mesh.devices.reshape(4, 8, 4), ("lat", "j", "m"))
    return jax.shard_map(
        per_device,
        mesh=inner,
        in_specs=(P("lat", LON, None),) + (P(),) * 12,
        out_specs=P("lat", LON, None),
        check_vma=False,
    )
```

time: 174 us -> 157 us (0.902)
  Pallas kernels: 83.8 us -> 56.1 us
  blocking collectives: 0 us -> 25.6 us
  starting transfers between devices: 45.6 us -> 27.7 us
  waiting for transfers between devices: 31.9 us -> 38.8 us
  other arithmetic: 6.09 us -> 1.03 us
    pallas_call x4, Pallas kernels: 83.8 us -> 56.1 us  [the longest x2 41.3 us: local_stage(): pl.pallas_call(functools.partial(local_kernel, blocks), in_specs=[vmem] *...]
    all_to_all x0 -> x1, blocking collectives: none -> 25.6 us  [per_device(): lax.all_to_all(parcels.reshape(shape), ('lat', 'j'), 0, 0, tiled=True)]
    all_to_all x4 -> x3, starting transfers between devices: 31.6 us -> 13.7 us  [the longest x2 9.18 us: per_device(): back = lax.all_to_all(groups.reshape(shape), ('lat', 'j'), 0, 0, tiled=True)]
    all_to_all x4 -> x3, waiting for transfers between devices: 29.7 us -> 38.8 us  [the longest x2 28.3 us: per_device(): back = lax.all_to_all(groups.reshape(shape), ('lat', 'j'), 0, 0, tiled=True)]
    slice x4 -> x3, local copies, waits for them, and re-layouts: 2.43 us -> 0.09 us  [the longest x1 0.08 us: per_device(): whole = jnp.concatenate([outer[:, :, :8], inner, outer[:, :, 8:]], axis=2)]
    ppermute x4, waiting for transfers between devices: 2.13 us -> 0.01 us  [shift(): return lax.ppermute(values, axis, pairs)]
  transfers between devices with their start and end apart: 8 -> 7, of which waited for: 4 -> 3; matrix products, arithmetic and copies ran while one was open for 5% -> 2% of each run, Pallas kernels for 31% -> 23%
where the time goes in v1:
time: 157 us; the launch traced here: 155 us
  Pallas kernels  56.1 us (36%)
  waiting for transfers between devices  38.8 us (25%)
  starting transfers between devices  27.7 us (18%)
  blocking collectives  25.6 us (16%)
  local copies, waits for them, and re-layouts  5.32 us (3%)
    pallas_call x2, Pallas kernels, local_stage(): pl.pallas_call(functools.partial(local_kernel, blocks), in_specs=[vmem] *...  41.3 us
    all_to_all x2, waiting for transfers between devices, per_device(): back = lax.all_to_all(groups.reshape(shape), ('lat', 'j'), 0, 0, tiled=True)  28.3 us
    all_to_all x1, blocking collectives, per_device(): lax.all_to_all(parcels.reshape(shape), ('lat', 'j'), 0, 0, tiled=True)  25.6 us
    pallas_call x2, Pallas kernels, grid_stage(): pl.pallas_call(grid_kernel, grid=(rows,), in_specs=[block] + [whole(w) fo...  14.8 us
    ppermute x4, starting transfers between devices, shift(): return lax.ppermute(values, axis, pairs)  14 us
    all_to_all x1, waiting for transfers between devices, per_device(): lax.all_to_all(parcels.reshape(shape), ('lat', 'j'), 0, 0, tiled=True)  10.5 us
    all_to_all x2, starting transfers between devices, per_device(): back = lax.all_to_all(groups.reshape(shape), ('lat', 'j'), 0, 0, tiled=True)  9.18 us
    all_to_all x1, starting transfers between devices, per_device(): lax.all_to_all(parcels.reshape(shape), ('lat', 'j'), 0, 0, tiled=True)  4.55 us
  transfers between devices with their start and end apart: 7, of which 3 were waited for; matrix products, arithmetic and copies ran while one was open for 2% of the time, Pallas kernels for 23%

profile of v1, /device:TPU:1, one launch (start us, length us, event | category | flops | bytes accessed | tf_op | source)
XLA Modules:
  0.0 154.8 jit_solution(17321085856728964417)
XLA Ops:
  0.0 0.7 fusion.1
  0.7 3.3 %collective-permute-start.1 = (bf16[1,32,256]{2,1,0:T(8,128)(2,1)S(1)}, bf16[1,32,256]{2,1,0:T(8,128)(2,1)S(1)}, u32[]{:S(2)}, u32[]{:S(2)}) collective-permute-start(bf16[1,32,256]{2,1,0:T(8,128)(2,1)S(1)} %get-tuple-element.11), channel_id=1, source_target_pairs={{32,0},{64,32},{96,64},{33,1},{65,33},{97,65},{34,2},{66,34},{98,6... | collective-permute-start | bytes 49160 | tf_op jit(solution)/shard_map/ppermute | solution.py:306
  4.1 3.5 %collective-permute-start = (bf16[1,32,256]{2,1,0:T(8,128)(2,1)S(1)}, bf16[1,32,256]{2,1,0:T(8,128)(2,1)S(1)}, u32[]{:S(2)}, u32[]{:S(2)}) collective-permute-start(bf16[1,32,256]{2,1,0:T(8,128)(2,1)S(1)} %get-tuple-element.12), channel_id=1, source_target_pairs={{0,32},{32,64},{64,96},{1,33},{33,65},{65,97},{2,34},{34,66},{66,9... | collective-permute-start | bytes 49160 | tf_op jit(solution)/shard_map/ppermute | solution.py:306
  7.6 1.4 fusion
  9.0 1.4 reshape.38.refs_3_.refs_4_
  10.5 0.0 collective-permute-done.1.south_ref
  10.5 0.0 copy-start.1
  10.5 0.0 collective-permute-done.north_ref
  10.5 0.0 copy-start.2
  10.6 1.3 collective-permute-start.3
  11.9 5.8 %collective-permute-start.2 = (bf16[130,256]{1,0:T(8,128)(2,1)S(1)}, bf16[130,256]{1,0:T(8,128)(2,1)S(1)}, u32[]{:S(2)}, u32[]{:S(2)}) collective-permute-start(bf16[130,256]{1,0:T(8,128)(2,1)S(1)} %pad_maximum_fusion.1), channel_id=1, source_target_pairs={{0,1},{1,2},{2,3},{3,4},{4,5},{5,6},{6,7},{7,8},{8,9},{9,10},{10,1... | collective-permute-start | bytes 199688 | tf_op jit(solution)/shard_map/ppermute | solution.py:306
  17.8 0.0 copy-done.1
  17.8 0.0 copy-done.2
  17.8 20.4 %local_stage.2 = bf16[64,2,16,256]{3,2,1,0:T(8,128)(2,1)} custom-call(bf16[128,32,256]{2,1,0:T(8,128)(2,1)} %field_ref.3, bf16[1,32,256]{2,1,0:T(8,128)(2,1)} %copy-done.2, bf16[1,32,256]{2,1,0:T(8,128)(2,1)} %copy-done.1, f32[1,256]{1,0:T(1,128)} %bitcast.65, bf16[256,1024]{1,0:T(8,128)(2,1)} %refs_2_.1, f32[1,1024]{1,0:T(1,128)} %bitcast.61, ...), custom_call_target="tpu_custom_call" | custom-call | flops 5000000000 | bytes 3000000 | tf_op jit(solution)/shard_map/local_stage/pallas_call | solution.py:249
  38.2 0.0 collective-permute-done.3
  38.3 0.0 collective-permute-done.2
  38.4 0.7 maximum_maximum_fusion.refs_0_
  39.0 20.9 %local_stage.3 = bf16[64,2,16,256]{3,2,1,0:T(8,128)(2,1)} custom-call(bf16[128,32,256]{2,1,0:T(8,128)(2,1)} %field_ref.3, bf16[1,32,256]{2,1,0:T(8,128)(2,1)} %copy-done.2, bf16[1,32,256]{2,1,0:T(8,128)(2,1)} %copy-done.1, bf16[10,32,256]{2,1,0:T(8,128)(2,1)} %maximum_maximum_fusion.refs_0_, f32[1,256]{1,0:T(1,128)} %bitcast.66, bf16[256,1024]{1,0:T(8,128)(2,1)} %refs_2_.1, ...), custom_call_target="tpu_custom_call" | custom-call | flops 5000000000 | bytes 3000000 | tf_op jit(solution)/shard_map/local_stage/pallas_call | solution.py:249
  59.9 25.6 %all_to_all.20 = bf16[32,64,256]{2,1,0:T(8,128)(2,1)} all-to-all(bf16[32,64,256]{2,1,0:T(8,128)(2,1)} %bitcast.54), channel_id=1, replica_groups=mesh['lat'=4,'j'=8,'m'=4] {'lat','j'}, dimensions={0} | all-to-all | bytes 2097152 | tf_op jit(solution)/shard_map/all_to_all | solution.py:361
  85.5 4.5 %all-to-all-start.2 = ((bf16[32,64,256]{2,1,0:T(8,128)(2,1)}), bf16[32,64,256]{2,1,0:T(8,128)(2,1)S(1)}, u32[]{:S(2)}, u32[]{:S(2)}) async-start(bf16[32,64,256]{2,1,0:T(8,128)(2,1)} %bitcast.23), calls=%async_computation.2 | async-start | bytes 2097152 | tf_op jit(solution)/shard_map/all_to_all | solution.py:361
  90.1 7.4 %grid_stage.2 = bf16[32,2,2,16,256]{4,3,2,1,0:T(8,128)(2,1)} custom-call(bf16[32,2,2,16,256]{4,3,2,1,0:T(8,128)(2,1)} %bitcast.53, f32[1,256]{1,0:T(1,128)} %bitcast.69, bf16[256,768]{1,0:T(8,128)(2,1)} %w_qkv_ref.3, bf16[256,256]{1,0:T(8,128)(2,1)} %w_out_ref.3), custom_call_target="tpu_custom_call" | custom-call | flops 3000000000 | bytes 2500000 | tf_op jit(solution)/shard_map/grid_stage/pallas_call | solution.py:288
  97.5 10.5 %all-to-all-done.2 = bf16[32,64,256]{2,1,0:T(8,128)(2,1)S(1)} async-done(((bf16[32,64,256]{2,1,0:T(8,128)(2,1)}), bf16[32,64,256]{2,1,0:T(8,128)(2,1)S(1)}, u32[]{:S(2)}, u32[]{:S(2)}) %all-to-all-start.2) | async-done | bytes 1048608 | tf_op jit(solution)/shard_map/all_to_all | solution.py:361
  108.0 0.0 copy-start
  108.0 4.6 %all-to-all-start.1 = ((bf16[32,64,256]{2,1,0:T(8,128)(2,1)}), bf16[32,64,256]{2,1,0:T(8,128)(2,1)S(1)}, u32[]{:S(2)}, u32[]{:S(2)}) async-start(bf16[32,64,256]{2,1,0:T(8,128)(2,1)} %bitcast.52), calls=%async_computation.1 | async-start | bytes 2097152 | tf_op jit(solution)/shard_map/all_to_all | solution.py:366
  112.6 0.0 copy-done
  112.6 7.4 %grid_stage.3 = bf16[32,2,2,16,256]{4,3,2,1,0:T(8,128)(2,1)} custom-call(bf16[32,2,2,16,256]{4,3,2,1,0:T(8,128)(2,1)} %bitcast.50, f32[1,256]{1,0:T(1,128)} %bitcast.70, bf16[256,768]{1,0:T(8,128)(2,1)} %w_qkv_ref.3, bf16[256,256]{1,0:T(8,128)(2,1)} %w_out_ref.3), custom_call_target="tpu_custom_call" | custom-call | flops 3000000000 | bytes 2500000 | tf_op jit(solution)/shard_map/grid_stage/pallas_call | solution.py:288
  120.0 10.5 %all-to-all-done.1 = bf16[32,64,256]{2,1,0:T(8,128)(2,1)S(1)} async-done(((bf16[32,64,256]{2,1,0:T(8,128)(2,1)}), bf16[32,64,256]{2,1,0:T(8,128)(2,1)S(1)}, u32[]{:S(2)}, u32[]{:S(2)}) %all-to-all-start.1) | async-done | bytes 1048608 | tf_op jit(solution)/shard_map/all_to_all | solution.py:366
  130.5 4.6 %all-to-all-start.3 = ((bf16[32,64,256]{2,1,0:T(8,128)(2,1)}), bf16[32,64,256]{2,1,0:T(8,128)(2,1)S(1)}, u32[]{:S(2)}, u32[]{:S(2)}) async-start(bf16[32,64,256]{2,1,0:T(8,128)(2,1)} %bitcast.51), calls=%async_computation.3 | async-start | bytes 2097152 | tf_op jit(solution)/shard_map/all_to_all | solution.py:366
  135.0 0.1 fusion.2
  135.1 17.8 %all-to-all-done.3 = bf16[32,64,256]{2,1,0:T(8,128)(2,1)S(1)} async-done(((bf16[32,64,256]{2,1,0:T(8,128)(2,1)}), bf16[32,64,256]{2,1,0:T(8,128)(2,1)S(1)}, u32[]{:S(2)}, u32[]{:S(2)}) %all-to-all-start.3) | async-done | bytes 1048608 | tf_op jit(solution)/shard_map/all_to_all | solution.py:366
  152.9 0.3 pad_maximum_fusion
  153.2 1.5 copy.28
  (14 shorter events, 0.2 us)
Async XLA Ops:
  0.7 9.8 %collective-permute-start.1 = (bf16[1,32,256]{2,1,0:T(8,128)(2,1)S(1)}, bf16[1,32,256]{2,1,0:T(8,128)(2,1)S(1)}, u32[]{:S(2)}, u32[]{:S(2)}) collective-permute-start(bf16[1,32,256]{2,1,0:T(8,128)(2,1)S(1)} %get-tuple-element.11), channel_id=1, source_target_pairs={{32,0},{64,32},{96,64},{33,1},{65,33},{97,65},{34,2},{66,34},{98,6... | collective-permute-start | bytes 49160 | tf_op jit(solution)/shard_map/ppermute | solution.py:306
  4.1 6.5 %collective-permute-start = (bf16[1,32,256]{2,1,0:T(8,128)(2,1)S(1)}, bf16[1,32,256]{2,1,0:T(8,128)(2,1)S(1)}, u32[]{:S(2)}, u32[]{:S(2)}) collective-permute-start(bf16[1,32,256]{2,1,0:T(8,128)(2,1)S(1)} %get-tuple-element.12), channel_id=1, source_target_pairs={{0,32},{32,64},{64,96},{1,33},{33,65},{65,97},{2,34},{34,66},{66,9... | collective-permute-start | bytes 49160 | tf_op jit(solution)/shard_map/ppermute | solution.py:306
  10.5 7.3 %copy-start.1 = (bf16[1,32,256]{2,1,0:T(8,128)(2,1)}, bf16[1,32,256]{2,1,0:T(8,128)(2,1)S(1)}, u32[]{:S(2)}) copy-start(bf16[1,32,256]{2,1,0:T(8,128)(2,1)S(1)} %collective-permute-done.1.south_ref) | copy-start | bytes 49156
  10.5 7.2 %copy-start.2 = (bf16[1,32,256]{2,1,0:T(8,128)(2,1)}, bf16[1,32,256]{2,1,0:T(8,128)(2,1)S(1)}, u32[]{:S(2)}) copy-start(bf16[1,32,256]{2,1,0:T(8,128)(2,1)S(1)} %collective-permute-done.north_ref) | copy-start | bytes 49156
  10.6 27.6 %collective-permute-start.3 = (bf16[130,256]{1,0:T(8,128)(2,1)S(1)}, bf16[130,256]{1,0:T(8,128)(2,1)S(1)}, u32[]{:S(2)}, u32[]{:S(2)}) collective-permute-start(bf16[130,256]{1,0:T(8,128)(2,1)S(1)} %pad_maximum_fusion.2), channel_id=1, source_target_pairs={{1,0},{2,1},{3,2},{4,3},{5,4},{6,5},{7,6},{8,7},{9,8},{10,9},{11,1... | collective-permute-start | bytes 199688 | tf_op jit(solution)/shard_map/ppermute | solution.py:306
  11.9 26.3 %collective-permute-start.2 = (bf16[130,256]{1,0:T(8,128)(2,1)S(1)}, bf16[130,256]{1,0:T(8,128)(2,1)S(1)}, u32[]{:S(2)}, u32[]{:S(2)}) collective-permute-start(bf16[130,256]{1,0:T(8,128)(2,1)S(1)} %pad_maximum_fusion.1), channel_id=1, source_target_pairs={{0,1},{1,2},{2,3},{3,4},{4,5},{5,6},{6,7},{7,8},{8,9},{9,10},{10,1... | collective-permute-start | bytes 199688 | tf_op jit(solution)/shard_map/ppermute | solution.py:306
  85.5 22.5 %all-to-all-start.2 = ((bf16[32,64,256]{2,1,0:T(8,128)(2,1)}), bf16[32,64,256]{2,1,0:T(8,128)(2,1)S(1)}, u32[]{:S(2)}, u32[]{:S(2)}) async-start(bf16[32,64,256]{2,1,0:T(8,128)(2,1)} %bitcast.23), calls=%async_computation.2 | async-start | bytes 2097152 | tf_op jit(solution)/shard_map/all_to_all | solution.py:361
  108.0 4.6 %copy-start = (bf16[32,64,256]{2,1,0:T(8,128)(2,1)}, bf16[32,64,256]{2,1,0:T(8,128)(2,1)S(1)}, u32[]{:S(2)}) copy-start(bf16[32,64,256]{2,1,0:T(8,128)(2,1)S(1)} %all-to-all-done.2) | copy-start | bytes 3145732
  108.0 22.5 %all-to-all-start.1 = ((bf16[32,64,256]{2,1,0:T(8,128)(2,1)}), bf16[32,64,256]{2,1,0:T(8,128)(2,1)S(1)}, u32[]{:S(2)}, u32[]{:S(2)}) async-start(bf16[32,64,256]{2,1,0:T(8,128)(2,1)} %bitcast.52), calls=%async_computation.1 | async-start | bytes 2097152 | tf_op jit(solution)/shard_map/all_to_all | solution.py:366
  130.5 22.5 %all-to-all-start.3 = ((bf16[32,64,256]{2,1,0:T(8,128)(2,1)}), bf16[32,64,256]{2,1,0:T(8,128)(2,1)S(1)}, u32[]{:S(2)}, u32[]{:S(2)}) async-start(bf16[32,64,256]{2,1,0:T(8,128)(2,1)} %bitcast.51), calls=%async_computation.3 | async-start | bytes 2097152 | tf_op jit(solution)/shard_map/all_to_all | solution.py:366

commit v2 on v1

--- a/solution.py
+++ b/solution.py
@@ -182,7 +182,7 @@
                 acc_ref[128 * (r - 1) : 128 * r] = cells[16:144]
             normed_ref[160 * r : 160 * (r + 1)] = norm_rows(cells, gain_ref[...]).astype(BF16)
 
-        def channels(s, _):
+        def channels(s):
             at = pl.ds(pl.multiple_of(s * SLICE, SLICE), SLICE)
             bias = jnp.broadcast_to(b_expand_ref[:, at], (16, SLICE)).astype(BF16)
             bias = jnp.concatenate([bias] * 10, axis=0)
@@ -205,7 +205,7 @@
                 lanes = slice(128 * half, 128 * (half + 1))
                 there = pl.ds(pl.multiple_of(s * SLICE + 128 * half, 128), 128)
                 taps = [
-                    jnp.broadcast_to(0.5 * depth_ref[i : i + 1, there], (16, 128)).astype(BF16)
+                    jnp.broadcast_to(0.5 * depth_ref[i // 3, i % 3 : i % 3 + 1, there], (16, 128)).astype(BF16)
                     for i in range(9)
                 ]
                 depth_bias = jnp.broadcast_to(b_depth_ref[:, there], (16, 128)).astype(BF16)
@@ -225,9 +225,8 @@
                 w_project_ref[at, :] * jnp.asarray(0.5, BF16),
                 preferred_element_type=F32,
             )
-            return 0
-
-        lax.fori_loop(0, WIDE // SLICE, channels, 0)
+
+        lax.fori_loop(0, WIDE // SLICE, lambda s, c: (channels(s), c)[1], 0)
         mixed = acc_ref[...].astype(BF16)
         turned = [
             jnp.dot(swap, mixed[256 * i : 256 * (i + 1)], preferred_element_type=F32) for i in range(4)
@@ -265,7 +264,8 @@
     )(*arrays)
 
 
-def grid_kernel(in_ref, gain_ref, w_qkv_ref, w_out_ref, out_ref):
+def grid_kernel(in_ref, gain_ref, w_qkv_ref, w_out_ref, *refs):
+    out_ref = refs[-1]
     swap = swap_matrix()
     turned = []
     for c in range(4):
@@ -278,19 +278,22 @@
     for c in range(4):
         block = jnp.concatenate([done[64 * k + 16 * c : 64 * k + 16 * c + 16] for k in range(16)], axis=0)
         back = jnp.dot(swap, block, preferred_element_type=F32).astype(BF16)
-        out_ref[8 * c : 8 * c + 8] = back.reshape(8, 1, 2, 16, WIDTH)
-
-
-def grid_stage(landed, weights):
-    rows = landed.shape[1]
+        out_ref[8 * c : 8 * c + 8] = back.reshape(8, 1, 1, 2, 16, WIDTH)
+
+
+def grid_stage(part, landed, weights, done):
     whole = lambda a: pl.BlockSpec(a.shape, lambda r: (0,) * a.ndim)
     block = pl.BlockSpec((32, 1, 2, 16, WIDTH), lambda r: (0, r, 0, 0, 0))
+    more = () if done is None else (done,)
     return pl.pallas_call(
         grid_kernel,
-        grid=(rows,),
-        in_specs=[block] + [whole(w) for w in weights],
-        out_specs=block,
-        out_shape=jax.ShapeDtypeStruct(landed.shape, BF16),
+        grid=(2,),
+        in_specs=[block]
+        + [whole(w) for w in weights]
+        + [pl.BlockSpec(memory_space=pl.ANY)] * len(more),
+        out_specs=pl.BlockSpec((32, 1, 1, 2, 16, WIDTH), lambda r: (0, part, r, 0, 0, 0)),
+        out_shape=jax.ShapeDtypeStruct((32, 2, 2, 2, 16, WIDTH), BF16),
+        input_output_aliases={4: 0} if more else {},
         compiler_params=pltpu.CompilerParams(
             dimension_semantics=("arbitrary",), vmem_limit_bytes=VMEM_LIMIT
         ),
@@ -298,7 +301,7 @@
             flops=3_000_000_000, bytes_accessed=2_500_000, transcendentals=1_000_000
         ),
         name="grid_stage",
-    )(landed, *weights)
+    )(landed, *weights, *more)
 
 
 def shift(values, axis, step, count):
@@ -345,7 +348,7 @@
         norm_gain[None],
         expand_weight,
         expand_bias[None],
-        depth_kernel.reshape(9, WIDE),
+        depth_kernel,
         depth_bias[None],
         project_weight,
         block_gain[None],
@@ -354,18 +357,19 @@
     )
     grid_weights = (grid_gain[None], grid_qkv, grid_out)
     shape = (32, 64, WIDTH)
+    exchange = lambda parcels: lax.all_to_all(parcels.reshape(shape), ("lat", "j"), 0, 0, tiled=True)
     inner = local_stage((1, 2), field, north, south, None, local_weights)
-    sides, inner = lax.optimization_barrier((sides, inner))
+    inner_landed = exchange(inner)
+    sides, _ = lax.optimization_barrier((sides, inner))
     outer = local_stage((0, 3), field, north, south, sides, local_weights)
-    landed = [
-        lax.all_to_all(parcels.reshape(shape), ("lat", "j"), 0, 0, tiled=True) for parcels in (inner, outer)
-    ]
-    results = []
-    for groups in landed:
-        groups = grid_stage(groups.reshape(32, 2, 2, 16, WIDTH), grid_weights)
-        back = lax.all_to_all(groups.reshape(shape), ("lat", "j"), 0, 0, tiled=True)
-        results.append(back.reshape(64, 2, 16, WIDTH))
-    inner, outer = results
+    outer, _ = lax.optimization_barrier((outer, inner_landed))
+    outer_landed = exchange(outer)
+    pieces = (32, 2, 2, 16, WIDTH)
+    done = grid_stage(0, inner_landed.reshape(pieces), grid_weights, None)
+    done = grid_stage(1, outer_landed.reshape(pieces), grid_weights, done)
+    back = lax.all_to_all(done.reshape(32, 128, WIDTH), ("lat", "j"), 0, 0, tiled=True)
+    back = back.reshape(32, 2, 2, 2, 16, WIDTH)
+    inner, outer = (back[:, part].reshape(64, 2, 16, WIDTH) for part in range(2))
     whole = jnp.concatenate([outer[:, :, :8], inner, outer[:, :, 8:]], axis=2)
     return whole.transpose(1, 0, 2, 3).reshape(128, COLS, WIDTH)
 

time: 157 us -> 140 us (0.89)
  waiting for transfers between devices: 38.8 us -> 10.5 us
  blocking collectives: 25.6 us -> 33.8 us
  starting transfers between devices: 27.7 us -> 31 us
    all_to_all x2 -> x0, waiting for transfers between devices: 28.3 us -> none  [per_device(): back = lax.all_to_all(groups.reshape(shape), ('lat', 'j'), 0, 0, tiled=True)]
    all_to_all x1 -> x2, starting transfers between devices: 4.55 us -> 17.1 us  [per_device(): lax.all_to_all(parcels.reshape(shape), ('lat', 'j'), 0, 0, tiled=True)]
    all_to_all x2 -> x0, starting transfers between devices: 9.18 us -> none  [per_device(): back = lax.all_to_all(groups.reshape(shape), ('lat', 'j'), 0, 0, tiled=True)]
    all_to_all x1, blocking collectives: 25.6 us -> 33.8 us  [per_device(): lax.all_to_all(done.reshape(32, 128, WIDTH), ('lat', 'j'), 0, 0, tiled=True)]
    all_to_all x1 -> x2, waiting for transfers between devices: 10.5 us -> 10.4 us  [per_device(): lax.all_to_all(parcels.reshape(shape), ('lat', 'j'), 0, 0, tiled=True)]
  transfers between devices with their start and end apart: 7 -> 6, of which waited for: 3 -> 1; matrix products, arithmetic and copies ran while one was open for 2% -> 2% of each run, Pallas kernels for 23% -> 35%
where the time goes in v2:
time: 140 us; the launch traced here: 138 us
  Pallas kernels  55.9 us (40%)
  blocking collectives  33.8 us (24%)
  starting transfers between devices  31 us (22%)
  waiting for transfers between devices  10.5 us (8%)
  local copies, waits for them, and re-layouts  3.88 us (3%)
  other arithmetic  2.37 us (2%)
    pallas_call x2, Pallas kernels, local_stage(): pl.pallas_call(functools.partial(local_kernel, blocks), in_specs=[vmem] *...  41.1 us
    all_to_all x1, blocking collectives, per_device(): lax.all_to_all(done.reshape(32, 128, WIDTH), ('lat', 'j'), 0, 0, tiled=True)  33.8 us
    all_to_all x2, starting transfers between devices, per_device(): lax.all_to_all(parcels.reshape(shape), ('lat', 'j'), 0, 0, tiled=True)  17.1 us
    pallas_call x2, Pallas kernels, grid_stage(): pl.pallas_call(grid_kernel, grid=(2,), in_specs=[block] + [whole(w) for w...  14.8 us
    ppermute x4, starting transfers between devices, shift(): return lax.ppermute(values, axis, pairs)  14 us
    all_to_all x2, waiting for transfers between devices, per_device(): lax.all_to_all(parcels.reshape(shape), ('lat', 'j'), 0, 0, tiled=True)  10.4 us
  transfers between devices with their start and end apart: 6, of which 1 were waited for; matrix products, arithmetic and copies ran while one was open for 2% of the time, Pallas kernels for 35%

profile of v2, /device:TPU:1, one launch (start us, length us, event | category | flops | bytes accessed | tf_op | source)
XLA Modules:
  0.0 137.7 jit_solution(2009137994492884746)
XLA Ops:
  0.0 0.7 fusion.2
  0.7 3.3 %collective-permute-start.1 = (bf16[1,32,256]{2,1,0:T(8,128)(2,1)S(1)}, bf16[1,32,256]{2,1,0:T(8,128)(2,1)S(1)}, u32[]{:S(2)}, u32[]{:S(2)}) collective-permute-start(bf16[1,32,256]{2,1,0:T(8,128)(2,1)S(1)} %get-tuple-element.13), channel_id=1, source_target_pairs={{32,0},{64,32},{96,64},{33,1},{65,33},{97,65},{34,2},{66,34},{98,6... | collective-permute-start | bytes 49160 | tf_op jit(solution)/shard_map/ppermute | solution.py:309
  4.1 3.5 %collective-permute-start = (bf16[1,32,256]{2,1,0:T(8,128)(2,1)S(1)}, bf16[1,32,256]{2,1,0:T(8,128)(2,1)S(1)}, u32[]{:S(2)}, u32[]{:S(2)}) collective-permute-start(bf16[1,32,256]{2,1,0:T(8,128)(2,1)S(1)} %get-tuple-element.14), channel_id=1, source_target_pairs={{0,32},{32,64},{64,96},{1,33},{33,65},{65,97},{2,34},{34,66},{66,9... | collective-permute-start | bytes 49160 | tf_op jit(solution)/shard_map/ppermute | solution.py:309
  7.6 1.4 %fusion.1 = (bf16[128,1,256]{2,1,0:T(2,128)(2,1)S(1)}, bf16[128,1,256]{2,1,0:T(2,128)(2,1)S(1)}) fusion(bf16[128,32,256]{2,1,0:T(8,128)(2,1)} %field_ref.3), kind=kLoop, calls=%fused_computation.19 | loop fusion | bytes 262144 | tf_op jit(solution)/shard_map/slice | solution.py:335
  9.1 0.0 collective-permute-done.1.south_ref
  9.1 0.0 copy-start.2
  9.1 0.0 collective-permute-done.north_ref
  9.1 0.0 copy-start.3
  9.2 1.3 collective-permute-start.3
  10.5 5.8 %collective-permute-start.2 = (bf16[130,256]{1,0:T(8,128)(2,1)S(1)}, bf16[130,256]{1,0:T(8,128)(2,1)S(1)}, u32[]{:S(2)}, u32[]{:S(2)}) collective-permute-start(bf16[130,256]{1,0:T(8,128)(2,1)S(1)} %pad_maximum_fusion.1), channel_id=1, source_target_pairs={{0,1},{1,2},{2,3},{3,4},{4,5},{5,6},{6,7},{7,8},{8,9},{9,10},{10,1... | collective-permute-start | bytes 199688 | tf_op jit(solution)/shard_map/ppermute | solution.py:309
  16.3 0.0 copy-done.2
  16.3 0.0 copy-done.3
  16.4 20.4 %local_stage.2 = bf16[64,2,16,256]{3,2,1,0:T(8,128)(2,1)} custom-call(bf16[128,32,256]{2,1,0:T(8,128)(2,1)} %field_ref.3, bf16[1,32,256]{2,1,0:T(8,128)(2,1)} %copy-done.3, bf16[1,32,256]{2,1,0:T(8,128)(2,1)} %copy-done.2, f32[1,256]{1,0:T(1,128)} %bitcast.66, bf16[256,1024]{1,0:T(8,128)(2,1)} %refs_2_.1, f32[1,1024]{1,0:T(1,128)} %bitcast.62, ...), custom_call_target="tpu_custom_call" | custom-call | flops 5000000000 | bytes 3000000 | tf_op jit(solution)/shard_map/local_stage/pallas_call | solution.py:248
  36.7 8.8 %all-to-all-start = ((bf16[32,64,256]{2,1,0:T(8,128)(2,1)}), bf16[32,64,256]{2,1,0:T(8,128)(2,1)S(1)}, u32[]{:S(2)}, u32[]{:S(2)}) async-start(bf16[32,64,256]{2,1,0:T(8,128)(2,1)} %bitcast.53), calls=%async_computation | async-start | bytes 2097152 | tf_op jit(solution)/shard_map/all_to_all | solution.py:360
  45.5 0.0 collective-permute-done.3
  45.6 0.0 collective-permute-done.2
  45.7 0.7 maximum_maximum_fusion.refs_0_
  46.4 20.7 %local_stage.3 = bf16[64,2,16,256]{3,2,1,0:T(8,128)(2,1)} custom-call(bf16[128,32,256]{2,1,0:T(8,128)(2,1)} %field_ref.3, bf16[1,32,256]{2,1,0:T(8,128)(2,1)} %copy-done.3, bf16[1,32,256]{2,1,0:T(8,128)(2,1)} %copy-done.2, bf16[10,32,256]{2,1,0:T(8,128)(2,1)} %maximum_maximum_fusion.refs_0_, f32[1,256]{1,0:T(1,128)} %bitcast.67, bf16[256,1024]{1,0:T(8,128)(2,1)} %refs_2_.1, ...), custom_call_target="tpu_custom_call" | custom-call | flops 5000000000 | bytes 3000000 | tf_op jit(solution)/shard_map/local_stage/pallas_call | solution.py:248
  67.1 0.0 all-to-all-done
  67.1 0.0 copy-start
  67.1 8.3 %all-to-all-start.1 = ((bf16[32,64,256]{2,1,0:T(8,128)(2,1)}), bf16[32,64,256]{2,1,0:T(8,128)(2,1)S(1)}, u32[]{:S(2)}, u32[]{:S(2)}) async-start(bf16[32,64,256]{2,1,0:T(8,128)(2,1)} %bitcast.54), calls=%async_computation.1 | async-start | bytes 2097152 | tf_op jit(solution)/shard_map/all_to_all | solution.py:360
  75.4 0.0 copy-done
  75.4 7.4 %grid_stage.2.refs_0_ = bf16[32,2,2,2,16,256]{5,4,3,2,1,0:T(8,128)(2,1)} custom-call(bf16[32,2,2,16,256]{4,3,2,1,0:T(8,128)(2,1)} %bitcast.52, f32[1,256]{1,0:T(1,128)} %bitcast.70, bf16[256,768]{1,0:T(8,128)(2,1)} %w_qkv_ref.3, bf16[256,256]{1,0:T(8,128)(2,1)} %w_out_ref.3), custom_call_target="tpu_custom_call" | custom-call | flops 3000000000 | bytes 2500000 | tf_op jit(solution)/shard_map/grid_stage/pallas_call | solution.py:288
  82.8 10.4 %all-to-all-done.1 = bf16[32,64,256]{2,1,0:T(8,128)(2,1)S(1)} async-done(((bf16[32,64,256]{2,1,0:T(8,128)(2,1)}), bf16[32,64,256]{2,1,0:T(8,128)(2,1)S(1)}, u32[]{:S(2)}, u32[]{:S(2)}) %all-to-all-start.1) | async-done | bytes 1048608 | tf_op jit(solution)/shard_map/all_to_all | solution.py:360
  93.2 0.0 copy-start.1
  93.3 1.0 copy-done.1
  94.2 7.4 %grid_stage.3 = bf16[32,2,2,2,16,256]{5,4,3,2,1,0:T(8,128)(2,1)} custom-call(bf16[32,2,2,16,256]{4,3,2,1,0:T(8,128)(2,1)} %bitcast.55, f32[1,256]{1,0:T(1,128)} %bitcast.71, bf16[256,768]{1,0:T(8,128)(2,1)} %w_qkv_ref.3, bf16[256,256]{1,0:T(8,128)(2,1)} %w_out_ref.3, bf16[32,2,2,2,16,256]{5,4,3,2,1,0:T(8,128)(2,1)} %grid_stage.2.refs_0_), custom_call_target="tpu_custom_call", output_to_operand_aliasing={{}: (4, {})} | custom-call | flops 3000000000 | bytes 2500000 | tf_op jit(solution)/shard_map/grid_stage/pallas_call | solution.py:288
  101.6 33.8 %all_to_all.15 = bf16[32,128,256]{2,1,0:T(8,128)(2,1)S(1)} all-to-all(bf16[32,128,256]{2,1,0:T(8,128)(2,1)} %bitcast.51), channel_id=1, replica_groups=mesh['lat'=4,'j'=8,'m'=4] {'lat','j'}, dimensions={0} | all-to-all | bytes 4194304 | tf_op jit(solution)/shard_map/all_to_all | solution.py:370
  135.4 0.2 fusion
  135.7 0.1 copy.22
  135.8 0.1 copy.21
  136.0 0.1 fusion.3
  136.0 1.6 %pad_maximum_fusion = bf16[64,2,32,256]{3,2,0,1:T(8,128)(2,1)} fusion(bf16[64,2,8,256]{3,2,0,1:T(8,128)(2,1)S(1)} %get-tuple-element.16, bf16[64,2,16,256]{3,2,0,1:T(8,128)(2,1)S(1)} %bitcast.50, bf16[64,2,8,256]{3,2,0,1:T(8,128)(2,1)S(1)} %get-tuple-element.15), kind=kLoop, calls=%fused_computation | loop fusion | flops 6291456 | bytes 4194304 | tf_op jit(solution)/shard_map/concatenate | solution.py:373
  (14 shorter events, 0.2 us)
Async XLA Ops:
  0.7 8.3 %collective-permute-start.1 = (bf16[1,32,256]{2,1,0:T(8,128)(2,1)S(1)}, bf16[1,32,256]{2,1,0:T(8,128)(2,1)S(1)}, u32[]{:S(2)}, u32[]{:S(2)}) collective-permute-start(bf16[1,32,256]{2,1,0:T(8,128)(2,1)S(1)} %get-tuple-element.13), channel_id=1, source_target_pairs={{32,0},{64,32},{96,64},{33,1},{65,33},{97,65},{34,2},{66,34},{98,6... | collective-permute-start | bytes 49160 | tf_op jit(solution)/shard_map/ppermute | solution.py:309
  4.1 5.0 %collective-permute-start = (bf16[1,32,256]{2,1,0:T(8,128)(2,1)S(1)}, bf16[1,32,256]{2,1,0:T(8,128)(2,1)S(1)}, u32[]{:S(2)}, u32[]{:S(2)}) collective-permute-start(bf16[1,32,256]{2,1,0:T(8,128)(2,1)S(1)} %get-tuple-element.14), channel_id=1, source_target_pairs={{0,32},{32,64},{64,96},{1,33},{33,65},{65,97},{2,34},{34,66},{66,9... | collective-permute-start | bytes 49160 | tf_op jit(solution)/shard_map/ppermute | solution.py:309
  9.1 7.3 %copy-start.2 = (bf16[1,32,256]{2,1,0:T(8,128)(2,1)}, bf16[1,32,256]{2,1,0:T(8,128)(2,1)S(1)}, u32[]{:S(2)}) copy-start(bf16[1,32,256]{2,1,0:T(8,128)(2,1)S(1)} %collective-permute-done.1.south_ref) | copy-start | bytes 49156
  9.1 7.2 %copy-start.3 = (bf16[1,32,256]{2,1,0:T(8,128)(2,1)}, bf16[1,32,256]{2,1,0:T(8,128)(2,1)S(1)}, u32[]{:S(2)}) copy-start(bf16[1,32,256]{2,1,0:T(8,128)(2,1)S(1)} %collective-permute-done.north_ref) | copy-start | bytes 49156
  9.2 36.4 %collective-permute-start.3 = (bf16[130,256]{1,0:T(8,128)(2,1)S(1)}, bf16[130,256]{1,0:T(8,128)(2,1)S(1)}, u32[]{:S(2)}, u32[]{:S(2)}) collective-permute-start(bf16[130,256]{1,0:T(8,128)(2,1)S(1)} %pad_maximum_fusion.2), channel_id=1, source_target_pairs={{1,0},{2,1},{3,2},{4,3},{5,4},{6,5},{7,6},{8,7},{9,8},{10,9},{11,1... | collective-permute-start | bytes 199688 | tf_op jit(solution)/shard_map/ppermute | solution.py:309
  10.5 35.1 %collective-permute-start.2 = (bf16[130,256]{1,0:T(8,128)(2,1)S(1)}, bf16[130,256]{1,0:T(8,128)(2,1)S(1)}, u32[]{:S(2)}, u32[]{:S(2)}) collective-permute-start(bf16[130,256]{1,0:T(8,128)(2,1)S(1)} %pad_maximum_fusion.1), channel_id=1, source_target_pairs={{0,1},{1,2},{2,3},{3,4},{4,5},{5,6},{6,7},{7,8},{8,9},{9,10},{10,1... | collective-permute-start | bytes 199688 | tf_op jit(solution)/shard_map/ppermute | solution.py:309
  36.7 30.3 %all-to-all-start = ((bf16[32,64,256]{2,1,0:T(8,128)(2,1)}), bf16[32,64,256]{2,1,0:T(8,128)(2,1)S(1)}, u32[]{:S(2)}, u32[]{:S(2)}) async-start(bf16[32,64,256]{2,1,0:T(8,128)(2,1)} %bitcast.53), calls=%async_computation | async-start | bytes 2097152 | tf_op jit(solution)/shard_map/all_to_all | solution.py:360
  67.1 8.3 %copy-start = (bf16[32,64,256]{2,1,0:T(8,128)(2,1)}, bf16[32,64,256]{2,1,0:T(8,128)(2,1)S(1)}, u32[]{:S(2)}) copy-start(bf16[32,64,256]{2,1,0:T(8,128)(2,1)S(1)} %all-to-all-done) | copy-start | bytes 3145732
  67.1 26.2 %all-to-all-start.1 = ((bf16[32,64,256]{2,1,0:T(8,128)(2,1)}), bf16[32,64,256]{2,1,0:T(8,128)(2,1)S(1)}, u32[]{:S(2)}, u32[]{:S(2)}) async-start(bf16[32,64,256]{2,1,0:T(8,128)(2,1)} %bitcast.54), calls=%async_computation.1 | async-start | bytes 2097152 | tf_op jit(solution)/shard_map/all_to_all | solution.py:360
  93.2 1.0 copy-start.1

commit v3 on v2

--- a/solution.py
+++ b/solution.py
@@ -226,7 +226,12 @@
                 preferred_element_type=F32,
             )
 
-        lax.fori_loop(0, WIDE // SLICE, lambda s, c: (channels(s), c)[1], 0)
+        def two_slices(s, carry):
+            channels(2 * s)
+            channels(2 * s + 1)
+            return carry
+
+        lax.fori_loop(0, WIDE // SLICE // 2, two_slices, 0)
         mixed = acc_ref[...].astype(BF16)
         turned = [
             jnp.dot(swap, mixed[256 * i : 256 * (i + 1)], preferred_element_type=F32) for i in range(4)
@@ -277,23 +282,28 @@
     done = attend(tokens, gain_ref[...], w_qkv_ref[...], w_out_ref[...]).astype(BF16)
     for c in range(4):
         block = jnp.concatenate([done[64 * k + 16 * c : 64 * k + 16 * c + 16] for k in range(16)], axis=0)
-        back = jnp.dot(swap, block, preferred_element_type=F32).astype(BF16)
-        out_ref[8 * c : 8 * c + 8] = back.reshape(8, 1, 1, 2, 16, WIDTH)
-
-
-def grid_stage(part, landed, weights, done):
+        back = jnp.dot(swap, block, preferred_element_type=F32)
+        at = slice(8 * c, 8 * c + 8)
+        if len(refs) == 1:
+            out_ref[at] = back.astype(BF16).reshape(8, 1, 2, 16, WIDTH)
+        else:
+            back = back.reshape(16, 16, WIDTH)
+            inner = refs[0][at].astype(F32).reshape(16, 16, WIDTH)
+            rows = jnp.concatenate([back[:, :8], inner, back[:, 8:]], axis=1)
+            out_ref[at] = rows.astype(BF16).reshape(8, 1, 2, COLS, WIDTH)
+
+
+def grid_stage(landed, weights, inner):
     whole = lambda a: pl.BlockSpec(a.shape, lambda r: (0,) * a.ndim)
-    block = pl.BlockSpec((32, 1, 2, 16, WIDTH), lambda r: (0, r, 0, 0, 0))
-    more = () if done is None else (done,)
+    block = lambda n: pl.BlockSpec((32, 1, 2, n, WIDTH), lambda r: (0, r, 0, 0, 0))
+    more = () if inner is None else (inner,)
+    columns = COLS if more else 16
     return pl.pallas_call(
         grid_kernel,
         grid=(2,),
-        in_specs=[block]
-        + [whole(w) for w in weights]
-        + [pl.BlockSpec(memory_space=pl.ANY)] * len(more),
-        out_specs=pl.BlockSpec((32, 1, 1, 2, 16, WIDTH), lambda r: (0, part, r, 0, 0, 0)),
-        out_shape=jax.ShapeDtypeStruct((32, 2, 2, 2, 16, WIDTH), BF16),
-        input_output_aliases={4: 0} if more else {},
+        in_specs=[block(16)] + [whole(w) for w in weights] + [block(16)] * len(more),
+        out_specs=block(columns),
+        out_shape=jax.ShapeDtypeStruct((32, 2, 2, columns, WIDTH), BF16),
         compiler_params=pltpu.CompilerParams(
             dimension_semantics=("arbitrary",), vmem_limit_bytes=VMEM_LIMIT
         ),
@@ -365,13 +375,10 @@
     outer, _ = lax.optimization_barrier((outer, inner_landed))
     outer_landed = exchange(outer)
     pieces = (32, 2, 2, 16, WIDTH)
-    done = grid_stage(0, inner_landed.reshape(pieces), grid_weights, None)
-    done = grid_stage(1, outer_landed.reshape(pieces), grid_weights, done)
+    done = grid_stage(inner_landed.reshape(pieces), grid_weights, None)
+    done = grid_stage(outer_landed.reshape(pieces), grid_weights, done)
     back = lax.all_to_all(done.reshape(32, 128, WIDTH), ("lat", "j"), 0, 0, tiled=True)
-    back = back.reshape(32, 2, 2, 2, 16, WIDTH)
-    inner, outer = (back[:, part].reshape(64, 2, 16, WIDTH) for part in range(2))
-    whole = jnp.concatenate([outer[:, :, :8], inner, outer[:, :, 8:]], axis=2)
-    return whole.transpose(1, 0, 2, 3).reshape(128, COLS, WIDTH)
+    return back.reshape(64, 2, COLS, WIDTH).transpose(1, 0, 2, 3).reshape(128, COLS, WIDTH)
 
 
 def solution(mesh):

time: 140 us -> 135 us (0.964)
  Pallas kernels: 55.9 us -> 52.6 us
  other arithmetic: 2.37 us -> 0.74 us
    pallas_call x2, Pallas kernels: 41.1 us -> 37.3 us  [local_stage(): pl.pallas_call(functools.partial(local_kernel, blocks), in_specs=[vmem] *...]
    concatenate x1 -> x0, other arithmetic: 1.63 us -> none  [per_device(): whole = jnp.concatenate([outer[:, :, :8], inner, outer[:, :, 8:]], axis=2)]
    reshape x0 -> x1, local copies, waits for them, and re-layouts: none -> 1.49 us  [per_device(): back.reshape(64, 2, COLS, WIDTH).transpose(1, 0, 2, 3)]
  transfers between devices with their start and end apart: 6 -> 6, of which waited for: 1 -> 1; matrix products, arithmetic and copies ran while one was open for 2% -> 2% of each run, Pallas kernels for 35% -> 33%
where the time goes in v3:
time: 135 us; the launch traced here: 134 us
  Pallas kernels  52.6 us (39%)
  blocking collectives  33.8 us (25%)
  starting transfers between devices  31.1 us (23%)
  waiting for transfers between devices  10.4 us (8%)
  local copies, waits for them, and re-layouts  4.78 us (4%)
    pallas_call x2, Pallas kernels, local_stage(): pl.pallas_call(functools.partial(local_kernel, blocks), in_specs=[vmem] *...  37.3 us
    all_to_all x1, blocking collectives, per_device(): lax.all_to_all(done.reshape(32, 128, WIDTH), ('lat', 'j'), 0, 0, tiled=True)  33.8 us
    all_to_all x2, starting transfers between devices, per_device(): lax.all_to_all(parcels.reshape(shape), ('lat', 'j'), 0, 0, tiled=True)  17.1 us
    pallas_call x2, Pallas kernels, grid_stage(): pl.pallas_call(grid_kernel, grid=(2,), in_specs=[block(16)] + [whole(w) f...  15.2 us
    ppermute x4, starting transfers between devices, shift(): return lax.ppermute(values, axis, pairs)  14 us
    all_to_all x2, waiting for transfers between devices, per_device(): lax.all_to_all(parcels.reshape(shape), ('lat', 'j'), 0, 0, tiled=True)  10.4 us
  transfers between devices with their start and end apart: 6, of which 1 were waited for; matrix products, arithmetic and copies ran while one was open for 2% of the time, Pallas kernels for 33%

profile of v3, /device:TPU:1, one launch (start us, length us, event | category | flops | bytes accessed | tf_op | source)
XLA Modules:
  0.0 133.6 jit_solution(2787639213469036782)
XLA Ops:
  0.0 0.7 fusion.1
  0.7 3.3 %collective-permute-start.1 = (bf16[1,32,256]{2,1,0:T(8,128)(2,1)S(1)}, bf16[1,32,256]{2,1,0:T(8,128)(2,1)S(1)}, u32[]{:S(2)}, u32[]{:S(2)}) collective-permute-start(bf16[1,32,256]{2,1,0:T(8,128)(2,1)S(1)} %get-tuple-element.11), channel_id=1, source_target_pairs={{32,0},{64,32},{96,64},{33,1},{65,33},{97,65},{34,2},{66,34},{98,6... | collective-permute-start | bytes 49160 | tf_op jit(solution)/shard_map/ppermute | solution.py:319
  4.1 3.5 %collective-permute-start = (bf16[1,32,256]{2,1,0:T(8,128)(2,1)S(1)}, bf16[1,32,256]{2,1,0:T(8,128)(2,1)S(1)}, u32[]{:S(2)}, u32[]{:S(2)}) collective-permute-start(bf16[1,32,256]{2,1,0:T(8,128)(2,1)S(1)} %get-tuple-element.12), channel_id=1, source_target_pairs={{0,32},{32,64},{64,96},{1,33},{33,65},{65,97},{2,34},{34,66},{66,9... | collective-permute-start | bytes 49160 | tf_op jit(solution)/shard_map/ppermute | solution.py:319
  7.6 1.4 %fusion = (bf16[128,1,256]{2,1,0:T(2,128)(2,1)S(1)}, bf16[128,1,256]{2,1,0:T(2,128)(2,1)S(1)}) fusion(bf16[128,32,256]{2,1,0:T(8,128)(2,1)} %field_ref.3), kind=kLoop, calls=%fused_computation.17 | loop fusion | bytes 262144 | tf_op jit(solution)/shard_map/slice | solution.py:345
  9.1 0.0 collective-permute-done.1.south_ref
  9.1 0.0 copy-start.2
  9.1 0.0 collective-permute-done.north_ref
  9.1 0.0 copy-start.3
  9.2 1.3 collective-permute-start.3
  10.5 5.8 %collective-permute-start.2 = (bf16[130,256]{1,0:T(8,128)(2,1)S(1)}, bf16[130,256]{1,0:T(8,128)(2,1)S(1)}, u32[]{:S(2)}, u32[]{:S(2)}) collective-permute-start(bf16[130,256]{1,0:T(8,128)(2,1)S(1)} %pad_maximum_fusion), channel_id=1, source_target_pairs={{0,1},{1,2},{2,3},{3,4},{4,5},{5,6},{6,7},{7,8},{8,9},{9,10},{10,1... | collective-permute-start | bytes 199688 | tf_op jit(solution)/shard_map/ppermute | solution.py:319
  16.3 0.0 copy-done.2
  16.3 0.0 copy-done.3
  16.4 18.6 %local_stage.2 = bf16[64,2,16,256]{3,2,1,0:T(8,128)(2,1)} custom-call(bf16[128,32,256]{2,1,0:T(8,128)(2,1)} %field_ref.3, bf16[1,32,256]{2,1,0:T(8,128)(2,1)} %copy-done.3, bf16[1,32,256]{2,1,0:T(8,128)(2,1)} %copy-done.2, f32[1,256]{1,0:T(1,128)} %bitcast.62, bf16[256,1024]{1,0:T(8,128)(2,1)} %refs_2_.1, f32[1,1024]{1,0:T(1,128)} %bitcast.58, ...), custom_call_target="tpu_custom_call" | custom-call | flops 5000000000 | bytes 3000000 | tf_op jit(solution)/shard_map/local_stage/pallas_call | solution.py:253
  34.9 8.8 %all-to-all-start = ((bf16[32,64,256]{2,1,0:T(8,128)(2,1)}), bf16[32,64,256]{2,1,0:T(8,128)(2,1)S(1)}, u32[]{:S(2)}, u32[]{:S(2)}) async-start(bf16[32,64,256]{2,1,0:T(8,128)(2,1)} %bitcast.49), calls=%async_computation | async-start | bytes 2097152 | tf_op jit(solution)/shard_map/all_to_all | solution.py:370
  43.7 0.0 collective-permute-done.3
  43.8 0.0 collective-permute-done.2
  43.9 0.7 maximum_maximum_fusion.refs_0_
  44.6 18.8 %local_stage.3 = bf16[64,2,16,256]{3,2,1,0:T(8,128)(2,1)} custom-call(bf16[128,32,256]{2,1,0:T(8,128)(2,1)} %field_ref.3, bf16[1,32,256]{2,1,0:T(8,128)(2,1)} %copy-done.3, bf16[1,32,256]{2,1,0:T(8,128)(2,1)} %copy-done.2, bf16[10,32,256]{2,1,0:T(8,128)(2,1)} %maximum_maximum_fusion.refs_0_, f32[1,256]{1,0:T(1,128)} %bitcast.63, bf16[256,1024]{1,0:T(8,128)(2,1)} %refs_2_.1, ...), custom_call_target="tpu_custom_call" | custom-call | flops 5000000000 | bytes 3000000 | tf_op jit(solution)/shard_map/local_stage/pallas_call | solution.py:253
  63.3 0.0 all-to-all-done
  63.3 0.0 copy-start
  63.3 8.3 %all-to-all-start.1 = ((bf16[32,64,256]{2,1,0:T(8,128)(2,1)}), bf16[32,64,256]{2,1,0:T(8,128)(2,1)S(1)}, u32[]{:S(2)}, u32[]{:S(2)}) async-start(bf16[32,64,256]{2,1,0:T(8,128)(2,1)} %bitcast.50), calls=%async_computation.1 | async-start | bytes 2097152 | tf_op jit(solution)/shard_map/all_to_all | solution.py:370
  71.7 0.0 copy-done
  71.7 7.4 %grid_stage.2.refs_0_ = bf16[32,2,2,16,256]{4,3,2,1,0:T(8,128)(2,1)} custom-call(bf16[32,2,2,16,256]{4,3,2,1,0:T(8,128)(2,1)} %bitcast.48, f32[1,256]{1,0:T(1,128)} %bitcast.66, bf16[256,768]{1,0:T(8,128)(2,1)} %w_qkv_ref.3, bf16[256,256]{1,0:T(8,128)(2,1)} %w_out_ref.3), custom_call_target="tpu_custom_call" | custom-call | flops 3000000000 | bytes 2500000 | tf_op jit(solution)/shard_map/grid_stage/pallas_call | solution.py:301
  79.1 10.4 %all-to-all-done.1 = bf16[32,64,256]{2,1,0:T(8,128)(2,1)S(1)} async-done(((bf16[32,64,256]{2,1,0:T(8,128)(2,1)}), bf16[32,64,256]{2,1,0:T(8,128)(2,1)S(1)}, u32[]{:S(2)}, u32[]{:S(2)}) %all-to-all-start.1) | async-done | bytes 1048608 | tf_op jit(solution)/shard_map/all_to_all | solution.py:370
  89.5 0.0 copy-start.1
  89.5 1.0 copy-done.1
  90.5 7.8 %grid_stage.3 = bf16[32,2,2,32,256]{4,3,2,1,0:T(8,128)(2,1)} custom-call(bf16[32,2,2,16,256]{4,3,2,1,0:T(8,128)(2,1)} %bitcast.51, f32[1,256]{1,0:T(1,128)} %bitcast.67, bf16[256,768]{1,0:T(8,128)(2,1)} %w_qkv_ref.3, bf16[256,256]{1,0:T(8,128)(2,1)} %w_out_ref.3, bf16[32,2,2,16,256]{4,3,2,1,0:T(8,128)(2,1)} %grid_stage.2.refs_0_), custom_call_target="tpu_custom_call" | custom-call | flops 3000000000 | bytes 2500000 | tf_op jit(solution)/shard_map/grid_stage/pallas_call | solution.py:301
  98.3 33.8 %all_to_all.15 = bf16[32,128,256]{2,1,0:T(8,128)(2,1)S(1)} all-to-all(bf16[32,128,256]{2,1,0:T(8,128)(2,1)} %bitcast.47), channel_id=1, replica_groups=mesh['lat'=4,'j'=8,'m'=4] {'lat','j'}, dimensions={0} | all-to-all | bytes 4194304 | tf_op jit(solution)/shard_map/all_to_all | solution.py:380
  132.1 1.5 %copy.19 = bf16[64,2,32,256]{3,2,0,1:T(8,128)(2,1)} copy(bf16[64,2,32,256]{3,2,1,0:T(8,128)(2,1)S(1)} %bitcast.46) | data formatting | bytes 4194304 | tf_op jit(solution)/shard_map/reshape | solution.py:381
  (14 shorter events, 0.2 us)
Async XLA Ops:
  0.7 8.3 %collective-permute-start.1 = (bf16[1,32,256]{2,1,0:T(8,128)(2,1)S(1)}, bf16[1,32,256]{2,1,0:T(8,128)(2,1)S(1)}, u32[]{:S(2)}, u32[]{:S(2)}) collective-permute-start(bf16[1,32,256]{2,1,0:T(8,128)(2,1)S(1)} %get-tuple-element.11), channel_id=1, source_target_pairs={{32,0},{64,32},{96,64},{33,1},{65,33},{97,65},{34,2},{66,34},{98,6... | collective-permute-start | bytes 49160 | tf_op jit(solution)/shard_map/ppermute | solution.py:319
  4.1 5.0 %collective-permute-start = (bf16[1,32,256]{2,1,0:T(8,128)(2,1)S(1)}, bf16[1,32,256]{2,1,0:T(8,128)(2,1)S(1)}, u32[]{:S(2)}, u32[]{:S(2)}) collective-permute-start(bf16[1,32,256]{2,1,0:T(8,128)(2,1)S(1)} %get-tuple-element.12), channel_id=1, source_target_pairs={{0,32},{32,64},{64,96},{1,33},{33,65},{65,97},{2,34},{34,66},{66,9... | collective-permute-start | bytes 49160 | tf_op jit(solution)/shard_map/ppermute | solution.py:319
  9.1 7.3 %copy-start.2 = (bf16[1,32,256]{2,1,0:T(8,128)(2,1)}, bf16[1,32,256]{2,1,0:T(8,128)(2,1)S(1)}, u32[]{:S(2)}) copy-start(bf16[1,32,256]{2,1,0:T(8,128)(2,1)S(1)} %collective-permute-done.1.south_ref) | copy-start | bytes 49156
  9.1 7.2 %copy-start.3 = (bf16[1,32,256]{2,1,0:T(8,128)(2,1)}, bf16[1,32,256]{2,1,0:T(8,128)(2,1)S(1)}, u32[]{:S(2)}) copy-start(bf16[1,32,256]{2,1,0:T(8,128)(2,1)S(1)} %collective-permute-done.north_ref) | copy-start | bytes 49156
  9.2 34.5 %collective-permute-start.3 = (bf16[130,256]{1,0:T(8,128)(2,1)S(1)}, bf16[130,256]{1,0:T(8,128)(2,1)S(1)}, u32[]{:S(2)}, u32[]{:S(2)}) collective-permute-start(bf16[130,256]{1,0:T(8,128)(2,1)S(1)} %pad_maximum_fusion.1), channel_id=1, source_target_pairs={{1,0},{2,1},{3,2},{4,3},{5,4},{6,5},{7,6},{8,7},{9,8},{10,9},{11,1... | collective-permute-start | bytes 199688 | tf_op jit(solution)/shard_map/ppermute | solution.py:319
  10.5 33.3 %collective-permute-start.2 = (bf16[130,256]{1,0:T(8,128)(2,1)S(1)}, bf16[130,256]{1,0:T(8,128)(2,1)S(1)}, u32[]{:S(2)}, u32[]{:S(2)}) collective-permute-start(bf16[130,256]{1,0:T(8,128)(2,1)S(1)} %pad_maximum_fusion), channel_id=1, source_target_pairs={{0,1},{1,2},{2,3},{3,4},{4,5},{5,6},{6,7},{7,8},{8,9},{9,10},{10,1... | collective-permute-start | bytes 199688 | tf_op jit(solution)/shard_map/ppermute | solution.py:319
  34.9 28.4 %all-to-all-start = ((bf16[32,64,256]{2,1,0:T(8,128)(2,1)}), bf16[32,64,256]{2,1,0:T(8,128)(2,1)S(1)}, u32[]{:S(2)}, u32[]{:S(2)}) async-start(bf16[32,64,256]{2,1,0:T(8,128)(2,1)} %bitcast.49), calls=%async_computation | async-start | bytes 2097152 | tf_op jit(solution)/shard_map/all_to_all | solution.py:370
  63.3 8.3 %copy-start = (bf16[32,64,256]{2,1,0:T(8,128)(2,1)}, bf16[32,64,256]{2,1,0:T(8,128)(2,1)S(1)}, u32[]{:S(2)}) copy-start(bf16[32,64,256]{2,1,0:T(8,128)(2,1)S(1)} %all-to-all-done) | copy-start | bytes 3145732
  63.3 26.2 %all-to-all-start.1 = ((bf16[32,64,256]{2,1,0:T(8,128)(2,1)}), bf16[32,64,256]{2,1,0:T(8,128)(2,1)S(1)}, u32[]{:S(2)}, u32[]{:S(2)}) async-start(bf16[32,64,256]{2,1,0:T(8,128)(2,1)} %bitcast.50), calls=%async_computation.1 | async-start | bytes 2097152 | tf_op jit(solution)/shard_map/all_to_all | solution.py:370
  89.5 1.0 copy-start.1

commit v4 on v3

--- a/solution.py
+++ b/solution.py
@@ -239,10 +239,13 @@
         tokens = jnp.concatenate(
             [turned[i][16 * k : 16 * k + 16] for k in range(16) for i in range(4)], axis=0
         )
-        halves.append(attend(tokens, gain2_ref[...], w_qkv_ref[...], w_out_ref[...]))
+        halves.append(tokens)
+    done = attend(
+        jnp.concatenate(halves, axis=0), gain2_ref[...], w_qkv_ref[...], w_out_ref[...]
+    )
     for k in range(16):
         both = jnp.concatenate(
-            [halves[h][64 * k : 64 * k + 64].reshape(8, 8, WIDTH) for h in range(2)], axis=1
+            [done[1024 * h + 64 * k : 1024 * h + 64 * k + 64].reshape(8, 8, WIDTH) for h in range(2)], axis=1
         )
         out_ref[8 * (k % 8) : 8 * (k % 8) + 8, k // 8] = both.astype(BF16)
 

time: 135 us -> 134 us (level)
  Pallas kernels: 52.6 us -> 51.2 us
    pallas_call x2, Pallas kernels: 37.3 us -> 35.9 us  [local_stage(): pl.pallas_call(functools.partial(local_kernel, blocks), in_specs=[vmem] *...]
where the time goes in v4:
time: 134 us; the launch traced here: 132 us
  Pallas kernels  51.2 us (38%)
  blocking collectives  33.8 us (25%)
  starting transfers between devices  31 us (23%)
  waiting for transfers between devices  10.4 us (8%)
  local copies, waits for them, and re-layouts  4.78 us (4%)
    pallas_call x2, Pallas kernels, local_stage(): pl.pallas_call(functools.partial(local_kernel, blocks), in_specs=[vmem] *...  35.9 us
    all_to_all x1, blocking collectives, per_device(): lax.all_to_all(done.reshape(32, 128, WIDTH), ('lat', 'j'), 0, 0, tiled=True)  33.8 us
    all_to_all x2, starting transfers between devices, per_device(): lax.all_to_all(parcels.reshape(shape), ('lat', 'j'), 0, 0, tiled=True)  17.1 us
    pallas_call x2, Pallas kernels, grid_stage(): pl.pallas_call(grid_kernel, grid=(2,), in_specs=[block(16)] + [whole(w) f...  15.2 us
    ppermute x4, starting transfers between devices, shift(): return lax.ppermute(values, axis, pairs)  14 us
    all_to_all x2, waiting for transfers between devices, per_device(): lax.all_to_all(parcels.reshape(shape), ('lat', 'j'), 0, 0, tiled=True)  10.4 us
  transfers between devices with their start and end apart: 6, of which 1 were waited for; matrix products, arithmetic and copies ran while one was open for 2% of the time, Pallas kernels for 33%

profile of v4, /device:TPU:1, one launch (start us, length us, event | category | flops | bytes accessed | tf_op | source)
XLA Modules:
  0.0 132.2 jit_solution(10380616733962103564)
XLA Ops:
  0.0 0.7 fusion.1
  0.7 3.3 %collective-permute-start.1 = (bf16[1,32,256]{2,1,0:T(8,128)(2,1)S(1)}, bf16[1,32,256]{2,1,0:T(8,128)(2,1)S(1)}, u32[]{:S(2)}, u32[]{:S(2)}) collective-permute-start(bf16[1,32,256]{2,1,0:T(8,128)(2,1)S(1)} %get-tuple-element.11), channel_id=1, source_target_pairs={{32,0},{64,32},{96,64},{33,1},{65,33},{97,65},{34,2},{66,34},{98,6... | collective-permute-start | bytes 49160 | tf_op jit(solution)/shard_map/ppermute | solution.py:322
  4.1 3.5 %collective-permute-start = (bf16[1,32,256]{2,1,0:T(8,128)(2,1)S(1)}, bf16[1,32,256]{2,1,0:T(8,128)(2,1)S(1)}, u32[]{:S(2)}, u32[]{:S(2)}) collective-permute-start(bf16[1,32,256]{2,1,0:T(8,128)(2,1)S(1)} %get-tuple-element.12), channel_id=1, source_target_pairs={{0,32},{32,64},{64,96},{1,33},{33,65},{65,97},{2,34},{34,66},{66,9... | collective-permute-start | bytes 49160 | tf_op jit(solution)/shard_map/ppermute | solution.py:322
  7.6 1.4 %fusion = (bf16[128,1,256]{2,1,0:T(2,128)(2,1)S(1)}, bf16[128,1,256]{2,1,0:T(2,128)(2,1)S(1)}) fusion(bf16[128,32,256]{2,1,0:T(8,128)(2,1)} %field_ref.3), kind=kLoop, calls=%fused_computation.17 | loop fusion | bytes 262144 | tf_op jit(solution)/shard_map/slice | solution.py:348
  9.1 0.0 collective-permute-done.1.south_ref
  9.1 0.0 copy-start.2
  9.1 0.0 collective-permute-done.north_ref
  9.1 0.0 copy-start.3
  9.2 1.3 collective-permute-start.3
  10.5 5.8 %collective-permute-start.2 = (bf16[130,256]{1,0:T(8,128)(2,1)S(1)}, bf16[130,256]{1,0:T(8,128)(2,1)S(1)}, u32[]{:S(2)}, u32[]{:S(2)}) collective-permute-start(bf16[130,256]{1,0:T(8,128)(2,1)S(1)} %pad_maximum_fusion), channel_id=1, source_target_pairs={{0,1},{1,2},{2,3},{3,4},{4,5},{5,6},{6,7},{7,8},{8,9},{9,10},{10,1... | collective-permute-start | bytes 199688 | tf_op jit(solution)/shard_map/ppermute | solution.py:322
  16.3 0.0 copy-done.2
  16.3 0.0 copy-done.3
  16.4 17.8 %local_stage.2 = bf16[64,2,16,256]{3,2,1,0:T(8,128)(2,1)} custom-call(bf16[128,32,256]{2,1,0:T(8,128)(2,1)} %field_ref.3, bf16[1,32,256]{2,1,0:T(8,128)(2,1)} %copy-done.3, bf16[1,32,256]{2,1,0:T(8,128)(2,1)} %copy-done.2, f32[1,256]{1,0:T(1,128)} %bitcast.62, bf16[256,1024]{1,0:T(8,128)(2,1)} %refs_2_.1, f32[1,1024]{1,0:T(1,128)} %bitcast.58, ...), custom_call_target="tpu_custom_call" | custom-call | flops 5000000000 | bytes 3000000 | tf_op jit(solution)/shard_map/local_stage/pallas_call | solution.py:256
  34.2 8.8 %all-to-all-start = ((bf16[32,64,256]{2,1,0:T(8,128)(2,1)}), bf16[32,64,256]{2,1,0:T(8,128)(2,1)S(1)}, u32[]{:S(2)}, u32[]{:S(2)}) async-start(bf16[32,64,256]{2,1,0:T(8,128)(2,1)} %bitcast.49), calls=%async_computation | async-start | bytes 2097152 | tf_op jit(solution)/shard_map/all_to_all | solution.py:373
  42.9 0.0 collective-permute-done.3
  43.0 0.0 collective-permute-done.2
  43.1 0.7 maximum_maximum_fusion.refs_0_
  43.8 18.1 %local_stage.3 = bf16[64,2,16,256]{3,2,1,0:T(8,128)(2,1)} custom-call(bf16[128,32,256]{2,1,0:T(8,128)(2,1)} %field_ref.3, bf16[1,32,256]{2,1,0:T(8,128)(2,1)} %copy-done.3, bf16[1,32,256]{2,1,0:T(8,128)(2,1)} %copy-done.2, bf16[10,32,256]{2,1,0:T(8,128)(2,1)} %maximum_maximum_fusion.refs_0_, f32[1,256]{1,0:T(1,128)} %bitcast.63, bf16[256,1024]{1,0:T(8,128)(2,1)} %refs_2_.1, ...), custom_call_target="tpu_custom_call" | custom-call | flops 5000000000 | bytes 3000000 | tf_op jit(solution)/shard_map/local_stage/pallas_call | solution.py:256
  61.9 0.0 all-to-all-done
  61.9 0.0 copy-start
  61.9 8.3 %all-to-all-start.1 = ((bf16[32,64,256]{2,1,0:T(8,128)(2,1)}), bf16[32,64,256]{2,1,0:T(8,128)(2,1)S(1)}, u32[]{:S(2)}, u32[]{:S(2)}) async-start(bf16[32,64,256]{2,1,0:T(8,128)(2,1)} %bitcast.50), calls=%async_computation.1 | async-start | bytes 2097152 | tf_op jit(solution)/shard_map/all_to_all | solution.py:373
  70.2 0.0 copy-done
  70.3 7.4 %grid_stage.2.refs_0_ = bf16[32,2,2,16,256]{4,3,2,1,0:T(8,128)(2,1)} custom-call(bf16[32,2,2,16,256]{4,3,2,1,0:T(8,128)(2,1)} %bitcast.48, f32[1,256]{1,0:T(1,128)} %bitcast.66, bf16[256,768]{1,0:T(8,128)(2,1)} %w_qkv_ref.3, bf16[256,256]{1,0:T(8,128)(2,1)} %w_out_ref.3), custom_call_target="tpu_custom_call" | custom-call | flops 3000000000 | bytes 2500000 | tf_op jit(solution)/shard_map/grid_stage/pallas_call | solution.py:304
  77.7 10.4 %all-to-all-done.1 = bf16[32,64,256]{2,1,0:T(8,128)(2,1)S(1)} async-done(((bf16[32,64,256]{2,1,0:T(8,128)(2,1)}), bf16[32,64,256]{2,1,0:T(8,128)(2,1)S(1)}, u32[]{:S(2)}, u32[]{:S(2)}) %all-to-all-start.1) | async-done | bytes 1048608 | tf_op jit(solution)/shard_map/all_to_all | solution.py:373
  88.1 0.0 copy-start.1
  88.1 1.0 copy-done.1
  89.1 7.8 %grid_stage.3 = bf16[32,2,2,32,256]{4,3,2,1,0:T(8,128)(2,1)} custom-call(bf16[32,2,2,16,256]{4,3,2,1,0:T(8,128)(2,1)} %bitcast.51, f32[1,256]{1,0:T(1,128)} %bitcast.67, bf16[256,768]{1,0:T(8,128)(2,1)} %w_qkv_ref.3, bf16[256,256]{1,0:T(8,128)(2,1)} %w_out_ref.3, bf16[32,2,2,16,256]{4,3,2,1,0:T(8,128)(2,1)} %grid_stage.2.refs_0_), custom_call_target="tpu_custom_call" | custom-call | flops 3000000000 | bytes 2500000 | tf_op jit(solution)/shard_map/grid_stage/pallas_call | solution.py:304
  96.9 33.8 %all_to_all.15 = bf16[32,128,256]{2,1,0:T(8,128)(2,1)S(1)} all-to-all(bf16[32,128,256]{2,1,0:T(8,128)(2,1)} %bitcast.47), channel_id=1, replica_groups=mesh['lat'=4,'j'=8,'m'=4] {'lat','j'}, dimensions={0} | all-to-all | bytes 4194304 | tf_op jit(solution)/shard_map/all_to_all | solution.py:383
  130.7 1.5 %copy.19 = bf16[64,2,32,256]{3,2,0,1:T(8,128)(2,1)} copy(bf16[64,2,32,256]{3,2,1,0:T(8,128)(2,1)S(1)} %bitcast.46) | data formatting | bytes 4194304 | tf_op jit(solution)/shard_map/reshape | solution.py:384
  (14 shorter events, 0.2 us)
Async XLA Ops:
  0.7 8.3 %collective-permute-start.1 = (bf16[1,32,256]{2,1,0:T(8,128)(2,1)S(1)}, bf16[1,32,256]{2,1,0:T(8,128)(2,1)S(1)}, u32[]{:S(2)}, u32[]{:S(2)}) collective-permute-start(bf16[1,32,256]{2,1,0:T(8,128)(2,1)S(1)} %get-tuple-element.11), channel_id=1, source_target_pairs={{32,0},{64,32},{96,64},{33,1},{65,33},{97,65},{34,2},{66,34},{98,6... | collective-permute-start | bytes 49160 | tf_op jit(solution)/shard_map/ppermute | solution.py:322
  4.1 5.0 %collective-permute-start = (bf16[1,32,256]{2,1,0:T(8,128)(2,1)S(1)}, bf16[1,32,256]{2,1,0:T(8,128)(2,1)S(1)}, u32[]{:S(2)}, u32[]{:S(2)}) collective-permute-start(bf16[1,32,256]{2,1,0:T(8,128)(2,1)S(1)} %get-tuple-element.12), channel_id=1, source_target_pairs={{0,32},{32,64},{64,96},{1,33},{33,65},{65,97},{2,34},{34,66},{66,9... | collective-permute-start | bytes 49160 | tf_op jit(solution)/shard_map/ppermute | solution.py:322
  9.1 7.3 %copy-start.2 = (bf16[1,32,256]{2,1,0:T(8,128)(2,1)}, bf16[1,32,256]{2,1,0:T(8,128)(2,1)S(1)}, u32[]{:S(2)}) copy-start(bf16[1,32,256]{2,1,0:T(8,128)(2,1)S(1)} %collective-permute-done.1.south_ref) | copy-start | bytes 49156
  9.1 7.2 %copy-start.3 = (bf16[1,32,256]{2,1,0:T(8,128)(2,1)}, bf16[1,32,256]{2,1,0:T(8,128)(2,1)S(1)}, u32[]{:S(2)}) copy-start(bf16[1,32,256]{2,1,0:T(8,128)(2,1)S(1)} %collective-permute-done.north_ref) | copy-start | bytes 49156
  9.2 33.8 %collective-permute-start.3 = (bf16[130,256]{1,0:T(8,128)(2,1)S(1)}, bf16[130,256]{1,0:T(8,128)(2,1)S(1)}, u32[]{:S(2)}, u32[]{:S(2)}) collective-permute-start(bf16[130,256]{1,0:T(8,128)(2,1)S(1)} %pad_maximum_fusion.1), channel_id=1, source_target_pairs={{1,0},{2,1},{3,2},{4,3},{5,4},{6,5},{7,6},{8,7},{9,8},{10,9},{11,1... | collective-permute-start | bytes 199688 | tf_op jit(solution)/shard_map/ppermute | solution.py:322
  10.5 32.5 %collective-permute-start.2 = (bf16[130,256]{1,0:T(8,128)(2,1)S(1)}, bf16[130,256]{1,0:T(8,128)(2,1)S(1)}, u32[]{:S(2)}, u32[]{:S(2)}) collective-permute-start(bf16[130,256]{1,0:T(8,128)(2,1)S(1)} %pad_maximum_fusion), channel_id=1, source_target_pairs={{0,1},{1,2},{2,3},{3,4},{4,5},{5,6},{6,7},{7,8},{8,9},{9,10},{10,1... | collective-permute-start | bytes 199688 | tf_op jit(solution)/shard_map/ppermute | solution.py:322
  34.2 27.8 %all-to-all-start = ((bf16[32,64,256]{2,1,0:T(8,128)(2,1)}), bf16[32,64,256]{2,1,0:T(8,128)(2,1)S(1)}, u32[]{:S(2)}, u32[]{:S(2)}) async-start(bf16[32,64,256]{2,1,0:T(8,128)(2,1)} %bitcast.49), calls=%async_computation | async-start | bytes 2097152 | tf_op jit(solution)/shard_map/all_to_all | solution.py:373
  61.9 8.3 %copy-start = (bf16[32,64,256]{2,1,0:T(8,128)(2,1)}, bf16[32,64,256]{2,1,0:T(8,128)(2,1)S(1)}, u32[]{:S(2)}) copy-start(bf16[32,64,256]{2,1,0:T(8,128)(2,1)S(1)} %all-to-all-done) | copy-start | bytes 3145732
  61.9 26.2 %all-to-all-start.1 = ((bf16[32,64,256]{2,1,0:T(8,128)(2,1)}), bf16[32,64,256]{2,1,0:T(8,128)(2,1)S(1)}, u32[]{:S(2)}, u32[]{:S(2)}) async-start(bf16[32,64,256]{2,1,0:T(8,128)(2,1)} %bitcast.50), calls=%async_computation.1 | async-start | bytes 2097152 | tf_op jit(solution)/shard_map/all_to_all | solution.py:373
  88.1 1.0 copy-start.1
